TPU v7x, 128 devices: a whole 4x4x4 slice. The times are simulated.
128 devices in a mesh: chain: 128 (over z, y, x, core).
Axes of the slice: x: 4, y: 4, z: 4, core: 2. Of those that a mesh axis runs over, the one named last changes fastest.
Arguments:
- sketch: float32 [256, 64, 256], P('chain'), may hold values from -42 to 42
- inv_diag: float32 [256, 256, 256], P('chain'), may hold values from -0.1 to 1.5
- upper: float32 [256, 256, 256], P('chain'), may hold values from -1.5 to 1.5
- lower: float32 [256, 256, 256], P('chain'), may hold values from -1.1 to 1.1
Outputs:
- basis: float32 [256, 64, 256], P('chain')
- r_factor: float32 [64, 64], replicated
All inputs are finite; a program needn't handle non-finite values.
Results may differ from a plain program's by a relative error of at most 0.0003.
Values sent between devices are 32-bit elements; how exact they have to be, the bound alone decides.
A program may use at most 192 MiB of HBM per device.

v0:
```python
import jax
import jax.numpy as jnp
from jax import lax
from jax.sharding import PartitionSpec as P

HIGH = lax.Precision.HIGHEST


def carried_in(part, axis, combine, identity, reverse):
    count = lax.axis_size(axis)
    place = lax.axis_index(axis)
    ahead = count - 1 - place if reverse else place
    gathered = jax.tree.map(lambda a: lax.all_gather(a, axis), part)
    state = jax.tree.map(lambda a, e: jnp.zeros_like(a) + jnp.asarray(e, a.dtype), part, identity)

    def one(step, state):
        source = count - 1 - step if reverse else step
        return combine(
            state, jax.tree.map(lambda a: lax.dynamic_index_in_dim(a, source, 0, False), gathered)
        )

    return lax.fori_loop(0, ahead, one, state)


def product(left, right):
    return jnp.dot(left, right, precision=HIGH, preferred_element_type=jnp.float32)


def join_maps(earlier, later):
    return (product(earlier[0], later[0]), product(earlier[1], later[0]) + later[1])


def forward_step(state, blocks):
    rhs, coupling, inverse = blocks
    fresh = product(rhs - product(state, coupling), inverse)
    return (fresh, fresh)


def forward_compose_plain(acc, blocks):
    coupling, inverse = blocks
    return (-product(product(acc, coupling), inverse), None)


def backward_step(carry, blocks):
    state, coupling = blocks
    solved = state - carry
    return (product(solved, coupling), solved)


def backward_compose(acc, coupling):
    return (-product(acc, coupling), None)


def on_device(sketch, inv_diag, upper, lower):
    count = sketch.shape[0]
    columns = sketch.shape[1]
    width = sketch.shape[2]
    eye = jnp.eye(width, dtype=jnp.float32)
    blank = jnp.zeros((columns, width), jnp.float32)
    fwd_map, _ = lax.scan(forward_compose_plain, eye, (upper, inv_diag))
    fwd_end, zero_states = lax.scan(forward_step, blank, (sketch, upper, inv_diag))
    incoming = carried_in((fwd_map, fwd_end), "chain", join_maps, (eye, blank), False)[1]
    _, states = lax.scan(forward_step, incoming, (sketch, upper, inv_diag))
    back_map, _ = lax.scan(backward_compose, eye, lower, reverse=True)
    back_end, _ = lax.scan(backward_step, blank, (states, lower), reverse=True)
    from_above = carried_in((back_map, back_end), "chain", join_maps, (eye, blank), True)[1]
    _, solved = lax.scan(backward_step, from_above, (states, lower), reverse=True)
    local_gram = jnp.einsum("skb,slb->kl", solved, solved, precision=HIGH)
    total_gram = lax.psum(local_gram, "chain")
    gram = total_gram / (count * lax.axis_size("chain") * width)
    chol = jnp.linalg.cholesky(gram)
    identity = jnp.eye(columns, dtype=jnp.float32)
    inverse = lax.linalg.triangular_solve(chol, identity, left_side=True, lower=True)
    basis = jnp.einsum("kl,slb->skb", inverse, solved, precision=HIGH)
    return (basis, jnp.transpose(chol))


def solution(mesh):
    placed = (
        P("chain", None, None),
        P("chain", None, None),
        P("chain", None, None),
        P("chain", None, None),
    )
    return jax.shard_map(
        on_device,
        mesh=mesh,
        in_specs=placed,
        out_specs=(P("chain", None, None), P()),
        check_vma=False,
    )
```

profile of v0, /device:TPU:1, one launch (start us, length us, event | category | flops | bytes accessed | tf_op | source)
XLA Modules:
  0.0 677.5 jit_solution(16970784390179098600)
XLA Ops:
  7.2 4.9 while.104
  12.9 6.3 while.103
  12.9 1.5 fusion.96
  14.5 1.6 convolution_negate_fusion.3
  16.0 1.5 fusion.96
  17.6 1.6 convolution_negate_fusion.3
  20.1 3.2 while.102
  20.1 1.6 fusion.91
  21.7 1.6 fusion.91
  24.1 62.6 %all-gather.13.cloned.1.call-done = f32[8192,256]{1,0:T(8,128)} async-done(((f32[64,256]{1,0:T(8,128)}), f32[8192,256]{1,0:T(8,128)}) %all-gather.13.cloned.1.call-update) | async-done | bytes 8388624 | tf_op jit(solution)/shard_map/all_gather | solution.py:13
  86.7 107.3 %all-gather.11.cloned.1.call-done = f32[32768,256]{1,0:T(8,128)} async-done(((f32[256,256]{1,0:T(8,128)}), f32[32768,256]{1,0:T(8,128)}) %all-gather.11.cloned.1.call-update) | async-done | bytes 33554448 | tf_op jit(solution)/shard_map/all_gather | solution.py:13
  194.0 1.2 while.105
  195.3 4.9 while.106
  200.2 2.5 while.107
  203.4 118.0 %all-gather.9.cloned.1.call-done = f32[32768,256]{0,1:T(8,128)} async-done(((f32[256,256]{0,1:T(8,128)}), f32[32768,256]{0,1:T(8,128)}) %all-gather.9.cloned.1.call-update) | async-done | bytes 33554448 | tf_op jit(solution)/shard_map/all_gather | solution.py:13
  321.3 33.4 %copy.7 = f32[32768,256]{1,0:T(8,128)} copy(f32[32768,256]{0,1:T(8,128)} %all-gather.9.cloned.1.call-done) | data formatting | bytes 67108864 | tf_op jit(solution)/shard_map/all_gather | solution.py:13
  354.8 78.0 %all-gather.15.cloned.1.call-done = f32[8192,256]{1,0:T(8,128)} async-done(((f32[64,256]{1,0:T(8,128)}), f32[8192,256]{1,0:T(8,128)}) %all-gather.15.cloned.1.call-update) | async-done | bytes 8388624 | tf_op jit(solution)/shard_map/all_gather | solution.py:13
  432.8 160.3 %while.108 = (s32[]{:T(128)}, f32[64,256]{1,0:T(8,128)S(1)}, s32[]{:T(128)}, f32[128,256,256]{2,1,0:T(8,128)}, f32[128,64,256]{2,1,0:T(8,128)}, /*index=5*/s32[]{:T(128)}, s32[]{:T(128)}, s32[]{:T(128)}, s32[]{:T(128)}) while((s32[]{:T(128)}, f32[64,256]{1,0:T(8,128)S(1)}, s32[]{:T(128)}, f32[128,256,256]{2,1,0:T(8,128)}, ...), condition=%wide.region_13.14_spmd, body=%wide.region_12.13_spmd.sunk | while | flops 50348036 | bytes 590987 | solution.py:22
  432.8 1.2 fusion.114
  451.9 1.2 fusion.114
  453.2 1.2 fusion.114
  472.2 1.2 fusion.114
  473.5 1.2 fusion.114
  492.6 1.2 fusion.114
  512.9 1.2 fusion.114
  533.3 1.2 fusion.114
  534.6 1.2 fusion.114
  553.7 1.2 fusion.114
  574.0 1.2 fusion.114
  594.0 63.0 %psum.7 = f32[64,64]{0,1:T(8,128)S(1)} all-reduce(f32[64,64]{0,1:T(8,128)S(1)} %convolution_bitcast_fusion.6), channel_id=1, replica_groups=mesh['chain'=128] {'chain'}, use_global_device_ids=true, to_apply=%region_16.17 | all-reduce | flops 4096 | bytes 32768 | tf_op jit(solution)/shard_map/psum | solution.py:69
  657.1 5.8 cholesky.17
  664.2 4.9 custom-call.6
  (301 shorter events, 163.3 us)
Async XLA Ops:
  7.2 79.6 %all-gather.13.cloned.1.call-start = ((), (), s32[]{:S(2)}) async-start(), calls=%async_computation.2 | async-start | bytes 8454144 | tf_op jit(solution)/shard_map/all_gather | solution.py:13
  12.1 0.6 copy-start.3
  12.8 181.2 %all-gather.11.cloned.1.call-start = ((), (), s32[]{:S(2)}) async-start(), calls=%async_computation.1 | async-start | bytes 33816576 | tf_op jit(solution)/shard_map/all_gather | solution.py:13
  19.2 0.7 copy-start.2
  19.9 301.4 %all-gather.9.cloned.1.call-start = ((), (), s32[]{:S(2)}) async-start(), calls=%async_computation | async-start | bytes 33816576 | tf_op jit(solution)/shard_map/all_gather | solution.py:13
  23.3 0.7 copy-start.1
  24.0 408.7 %all-gather.15.cloned.1.call-start = ((), (), s32[]{:S(2)}) async-start(), calls=%async_computation.3 | async-start | bytes 8454144 | tf_op jit(solution)/shard_map/all_gather | solution.py:13
  202.7 0.6 copy-start.4
  203.4 389.7 %copy-start = (f32[2,256,256]{2,1,0:T(8,128)S(1)}, f32[2,256,256]{2,1,0:T(8,128)}, u32[]{:S(2)}) copy-start(f32[2,256,256]{2,1,0:T(8,128)} %get-tuple-element.950) | copy-start | bytes 1572868
Sparse Core Ops, SparseCore 0:
  12.9 73.7 all-gather.12
  89.7 104.2 all-gather.10
  196.9 124.4 all-gather.8
  324.7 107.9 all-gather.14
where the time goes:
time: 681 us; the launch traced here: 678 us
  waiting for transfers between devices  366 us (54%)
  matrix products  179 us (26%)
  blocking collectives  63 us (9%)
  local copies, waits for them, and re-layouts  37.9 us (6%)
  between operations  14 us (2%)
  other arithmetic  12.1 us (2%)
    all_gather x4, waiting for transfers between devices, carried_in(): gathered = jax.tree.map(lambda a: lax.all_gather(a, axis), part)  366 us
    dot_general x145, matrix products, product(): jnp.dot(left, right, precision=HIGH, preferred_element_type=jnp.float32)  178 us
    psum x1, blocking collectives, on_device(): total_gram = lax.psum(local_gram, 'chain')  63 us
    all_gather x1, local copies, waits for them, and re-layouts, carried_in(): gathered = jax.tree.map(lambda a: lax.all_gather(a, axis), part)  33.4 us
  transfers between devices with their start and end apart: 4, of which 4 were waited for; matrix products, arithmetic and copies ran while one was open for 8% of the time, Pallas kernels for 0%

commit v1 on v0

v1 whole, which is shorter than its diff:
```python
import jax
import jax.numpy as jnp
from jax import lax
from jax.experimental import pallas as pl
from jax.experimental.pallas import tpu as pltpu
from jax.sharding import PartitionSpec as P

HIGH = lax.Precision.HIGHEST
MESH = pl.DeviceIdType.MESH
F32 = jnp.float32

W = 256
K = 64
HALF_M = 128
HALF_C = 32
HALF = HALF_M + HALF_C
ROWS = 2 * HALF
SEMS = 72


def dot(a, b):
    return jnp.dot(a, b, precision=HIGH, preferred_element_type=F32)


def mat(n):
    return jnp.concatenate([n[0:HALF_M], n[HALF : HALF + HALF_M]], axis=0)


def vec(n):
    return jnp.concatenate([n[HALF_M:HALF], n[HALF + HALF_M : ROWS]], axis=0)


def pack(m, c):
    return jnp.concatenate([m[0:HALF_M], c[0:HALF_C], m[HALF_M:W], c[HALF_C:K]], axis=0)


def add_vec(r, n):
    return jnp.concatenate(
        [
            r[0:HALF_M],
            r[HALF_M:HALF] + n[HALF_M:HALF],
            r[HALF : HALF + HALF_M],
            r[HALF + HALF_M : ROWS] + n[HALF + HALF_M : ROWS],
        ],
        axis=0,
    )


def compose(f, n):
    return add_vec(dot(f, mat(n)), n)


def apply(v, n):
    return dot(v, mat(n)) + vec(n)


def identity(rows, columns):
    return (
        lax.broadcasted_iota(jnp.int32, (rows, columns), 0) == lax.broadcasted_iota(jnp.int32, (rows, columns), 1)
    ).astype(F32)


def factor(gram):
    work = jnp.concatenate([gram, identity(K, K)], axis=1)
    blocks = [work[8 * b : 8 * b + 8] for b in range(K // 8)]
    sub = lax.broadcasted_iota(jnp.int32, (8, 2 * K), 0)
    lane = lax.broadcasted_iota(jnp.int32, (8, 2 * K), 1)
    scale = [jnp.zeros((8, 2 * K), F32) for _ in range(K // 8)]
    for k in range(K):
        b, r = divmod(k, 8)
        row = jnp.broadcast_to(blocks[b][r : r + 1], (8, 2 * K))
        pivot = jnp.broadcast_to(row[:, k : k + 1], (8, 2 * K))
        scaled = row / pivot
        scale[b] = jnp.where(sub == r, pivot, scale[b])
        for i in range(b, K // 8):
            column = jnp.broadcast_to(blocks[i][:, k : k + 1], (8, 2 * K))
            if i == b:
                column = jnp.where(sub > r, column, 0.0)
            blocks[i] = blocks[i] - column * scaled
    out = jnp.concatenate([blocks[b] * lax.rsqrt(scale[b]) for b in range(K // 8)], axis=0)
    upper = jnp.where(
        lax.broadcasted_iota(jnp.int32, (K, K), 0) <= lax.broadcasted_iota(jnp.int32, (K, K), 1), out[:, 0:K], 0.0
    )
    return upper, out[:, K : 2 * K]


def kernel(
    sketch, inv_diag, upper, lower, basis, r_factor,
    own0, fc, gc, hc, y0s, y1s, dev_g, dev_h,
    xf, xg, xh, xpre, xsuf_h, xsuf_g, yf, yg, ypre, ysuf_g,
    zc, zm, zc_in, zm_in, va, va_in, zg, er, ep, ysuf_e, gsum, gx, gy, gz,
    send, recv,
):
    me = lax.axis_index("chain")
    c = lax.rem(me, 2)
    x = lax.rem(me // 2, 4)
    y = lax.rem(me // 8, 4)
    z = me // 32

    def at(zz, yy, xx, cc):
        return ((zz * 4 + yy) * 4 + xx) * 2 + cc

    sibling = at(z, y, x, 1 - c)
    xs = [at(z, y, lax.rem(x + k, 4), c) for k in range(4)]
    ys = [at(z, lax.rem(y + k, 4), x, c) for k in range(4)]
    zs = [at(lax.rem(z + k, 4), y, x, c) for k in range(4)]

    barrier = pltpu.get_barrier_semaphore()
    for other in (sibling, *xs[1:], *ys[1:], *zs[1:]):
        pl.semaphore_signal(barrier, inc=1, device_id=(other,), device_id_type=MESH)

    sent = []
    used = [0]

    def slot():
        used[0] += 1
        assert used[0] <= SEMS
        return used[0] - 1

    def start(src, dst, i, other):
        copy = pltpu.make_async_remote_copy(
            src_ref=src, dst_ref=dst, send_sem=send.at[i], recv_sem=recv.at[i], device_id=(other,), device_id_type=MESH
        )
        copy.start()
        sent.append(copy)

    def arrived(dst, i):
        pltpu.make_async_remote_copy(
            src_ref=dst, dst_ref=dst, send_sem=send.at[i], recv_sem=recv.at[i], device_id=(sibling,), device_id_type=MESH
        ).wait_recv()

    def half(ref, j, rows):
        return ref.at[j, pl.ds(pl.multiple_of(c * rows, 8), rows)]

    def other_half(ref, j, rows):
        return ref.at[j, pl.ds(pl.multiple_of((1 - c) * rows, 8), rows)]

    class Gather:
        def __init__(self, ref, rows, place, peers, steps):
            self.ref, self.rows, self.place, self.peers, self.steps = ref, rows, place, peers, steps
            self.first = {k: slot() for k in steps}
            self.second = {k: slot() for k in steps}

        def source(self, k):
            return lax.rem(self.place + 4 - k, 4)

        def start(self):
            for k in self.steps:
                part = half(self.ref, self.place, self.rows)
                start(part, part, self.first[k], self.peers[k])

        def forward(self):
            for k in self.steps:
                part = half(self.ref, self.source(k), self.rows)
                arrived(part, self.first[k])
                start(part, part, self.second[k], sibling)

        def finish(self):
            for k in self.steps:
                arrived(other_half(self.ref, self.source(k), self.rows), self.second[k])

    class Share:
        def __init__(self, ref, place, peers):
            self.ref, self.place, self.peers = ref, place, peers
            self.sems = {k: slot() for k in (1, 3, 2)}

        def start(self):
            for k in (1, 3, 2):
                start(self.ref.at[self.place], self.ref.at[self.place], self.sems[k], self.peers[k])

        def finish(self):
            for k in (1, 3, 2):
                arrived(self.ref.at[lax.rem(self.place + 4 - k, 4)], self.sems[k])

    y0s[...] = dot(pack(-upper[0], sketch[0]), inv_diag[0])
    own0[...] = dot(pack(-upper[1], sketch[1]), inv_diag[1])
    y1s[...] = compose(y0s[...], own0[...])
    fc[c] = y1s[...]
    pl.semaphore_wait(barrier, 10)
    sem_f, sem_g, sem_h = slot(), slot(), slot()
    start(fc.at[c], fc.at[c], sem_f, sibling)
    gc[c] = dot(lower[1], lower[0])
    start(gc.at[c], gc.at[c], sem_g, sibling)
    hc[c] = dot(y0s[...] - dot(y1s[...], lower[1]), lower[0])
    start(hc.at[c], hc.at[c], sem_h, sibling)
    arrived(fc.at[1 - c], sem_f)

    xf[x] = compose(fc[0], fc[1])
    gather_xf = Gather(xf, HALF, x, xs, (1, 3, 2))
    gather_xf.start()

    arrived(gc.at[1 - c], sem_g)
    arrived(hc.at[1 - c], sem_h)
    late = compose(fc[0], hc[1])
    xg[x] = dot(gc[1], gc[0])
    xh[x] = dot(late, gc[0]) + hc[0]
    second = c == 1
    dev_g[...] = jnp.where(second, identity(W, W), gc[1])
    dev_h[...] = jnp.where(second, 0.0, late)
    y0s[...] = jnp.where(second, compose(fc[0], y0s[...]), y0s[...])
    y1s[...] = jnp.where(second, xf[x], y1s[...])

    gather_xf.forward()
    gather_xf.finish()
    q01 = compose(xf[0], xf[1])
    xpre[2] = q01
    yf[y] = compose(q01, compose(xf[2], xf[3]))

    gather_yf = Gather(yf, HALF, y, ys, (1, 3, 2))
    gather_yf.start()
    gather_xg = Gather(xg, HALF_M, x, xs, (1, 3, 2))
    gather_xg.start()
    gather_xh = Gather(xh, HALF, x, xs, (1, 3, 2))
    gather_xh.start()

    eye = identity(W, W)
    xpre[0] = pack(eye, jnp.zeros((K, W), F32))
    xpre[1] = xf[0]
    xpre[3] = compose(xpre[2], xf[2])
    y0s[...] = compose(xpre[x], y0s[...])
    y1s[...] = compose(xpre[x], y1s[...])
    dev_h[...] = compose(xpre[x], dev_h[...])

    gather_yf.forward()
    gather_yf.finish()
    q01 = compose(yf[0], yf[1])
    ypre[2] = q01
    plane = compose(q01, compose(yf[2], yf[3]))

    zc[...] = vec(plane)
    zm[...] = mat(plane)
    sem_c, sem_m, sem_m2, sem_v1, sem_v2 = slot(), slot(), slot(), slot(), slot()
    start(zc, zc_in, sem_c, zs[1])

    def z_half(ref, which):
        return ref.at[pl.ds(pl.multiple_of(which * HALF_M, 8), HALF_M)]

    start(z_half(zm, c), z_half(zm_in, c), sem_m, zs[1])

    gather_xg.forward()
    gather_xg.finish()
    xsuf_g[3] = eye
    xsuf_g[2] = xg[3]
    xsuf_g[1] = dot(xg[3], xg[2])
    xsuf_g[0] = dot(xsuf_g[1], xg[1])
    yg[y] = dot(xsuf_g[0], xg[0])
    gather_yg = Gather(yg, HALF_M, y, ys, (1, 3, 2))
    gather_yg.start()

    arrived(zc_in, sem_c)
    va[...] = dot(zc_in[...], zm[...]) + zc[...]
    start(va, va_in.at[0], sem_v1, zs[1])
    start(va, va_in.at[1], sem_v2, zs[2])
    arrived(z_half(zm_in, c), sem_m)
    start(z_half(zm_in, c), z_half(zm_in, c), sem_m2, sibling)

    ypre[0] = pack(eye, jnp.zeros((K, W), F32))
    ypre[1] = yf[0]
    ypre[3] = compose(ypre[2], yf[2])

    gather_xh.forward()
    gather_xh.finish()
    xsuf_h[3] = jnp.zeros((ROWS, W), F32)
    xsuf_h[2] = compose(xpre[3], xh[3])
    xsuf_h[1] = dot(xsuf_h[2], xg[2]) + compose(xpre[2], xh[2])
    xsuf_h[0] = dot(xsuf_h[1], xg[1]) + compose(xf[0], xh[1])
    row_h = dot(xsuf_h[0], xg[0]) + xh[0]
    row_h = compose(ypre[y], row_h)

    arrived(z_half(zm_in, 1 - c), sem_m2)
    arrived(va_in.at[0], sem_v1)
    arrived(va_in.at[1], sem_v2)
    last = dot(va_in[1], zm_in[...]) + zc_in[...]
    entering = jnp.where(z == 0, 0.0, jnp.where(z == 1, zc_in[...], jnp.where(z == 2, va_in[0], last)))

    er[y] = apply(entering, row_h)
    share_er = Share(er, y, ys)
    share_er.start()

    entering = apply(entering, ypre[y])
    dev_h[...] = dot(xsuf_h[x], dev_g[...]) + dev_h[...]
    dev_g[...] = dot(xsuf_g[x], dev_g[...])
    x1 = apply(entering, y1s[...]) - apply(entering, dev_h[...])
    x0 = apply(entering, y0s[...]) - dot(x1, lower[1])

    gather_yg.forward()
    gather_yg.finish()
    ysuf_g[3] = eye
    ysuf_g[2] = yg[3]
    ysuf_g[1] = dot(yg[3], yg[2])
    ysuf_g[0] = dot(ysuf_g[1], yg[1])
    zg[z] = dot(ysuf_g[0], yg[0])
    gather_zg = Gather(zg, HALF_M, z, zs, (3, 2))
    gather_zg.start()

    share_er.finish()
    ysuf_e[3] = jnp.zeros((K, W), F32)
    ysuf_e[2] = er[3]
    ysuf_e[1] = dot(er[3], yg[2]) + er[2]
    ysuf_e[0] = dot(ysuf_e[1], yg[1]) + er[1]
    ep[z] = dot(ysuf_e[0], yg[0]) + er[0]

    share_ep = Share(ep, z, zs)
    share_ep.start()
    to_w1 = dot(ysuf_g[y], dev_g[...])
    to_w0 = dot(to_w1, lower[1])
    from_row = dot(ysuf_e[y], dev_g[...])
    x1 = x1 - from_row
    x0 = x0 + dot(from_row, lower[1])
    gather_zg.forward()
    gather_zg.finish()
    share_ep.finish()
    two = dot(ep[3], zg[2]) + ep[2]
    three = dot(two, zg[1]) + ep[1]
    entering = jnp.where(z == 3, 0.0, jnp.where(z == 2, ep[3], jnp.where(z == 1, two, three)))
    x1 = x1 - dot(entering, to_w1)
    x0 = x0 + dot(entering, to_w0)

    both = jnp.concatenate([x0, x1], axis=1)
    gram = lax.dot_general(both, both, (((1,), (1,)), ((), ())), precision=HIGH, preferred_element_type=F32)
    gsum[c] = jnp.concatenate([gram[0 : K // 2], gram[K // 2 : K]], axis=1)
    sem = slot()
    start(gsum.at[c], gsum.at[c], sem, sibling)
    arrived(gsum.at[1 - c], sem)
    gx[x] = gsum[0] + gsum[1]
    total = gx
    for ref, place, peers, after in ((gx, x, xs, (gy, y)), (gy, y, ys, (gz, z)), (gz, z, zs, None)):
        share = Share(ref, place, peers)
        share.start()
        share.finish()
        total = (ref[0] + ref[1]) + (ref[2] + ref[3])
        if after is not None:
            after[0][after[1]] = total
    total = total / (256 * W)
    gram = jnp.concatenate([total[:, 0:K], total[:, K : 2 * K]], axis=0)
    r, inverse = factor(gram)
    r_factor[...] = r
    basis[0] = dot(inverse, x0)
    basis[1] = dot(inverse, x1)
    for copy in sent:
        copy.wait_send()


def on_device(sketch, inv_diag, upper, lower):
    def buf(*shape):
        return pltpu.VMEM(shape, F32)

    affine = (ROWS, W)
    vmem = pl.BlockSpec(memory_space=pltpu.VMEM)
    scratch = [
        buf(*affine), buf(2, *affine), buf(2, W, W), buf(2, *affine), buf(*affine), buf(*affine), buf(W, W), buf(*affine),
        buf(4, *affine), buf(4, W, W), buf(4, *affine), buf(4, *affine), buf(4, *affine), buf(4, W, W),
        buf(4, *affine), buf(4, W, W), buf(4, *affine), buf(4, W, W),
        buf(K, W), buf(W, W), buf(K, W), buf(W, W), buf(K, W), buf(2, K, W), buf(4, W, W),
        buf(4, K, W), buf(4, K, W), buf(4, K, W),
        buf(2, K // 2, 2 * K), buf(4, K // 2, 2 * K), buf(4, K // 2, 2 * K), buf(4, K // 2, 2 * K),
        pltpu.SemaphoreType.DMA((SEMS,)), pltpu.SemaphoreType.DMA((SEMS,)),
    ]
    return pl.pallas_call(
        kernel,
        out_shape=(jax.ShapeDtypeStruct((2, K, W), F32), jax.ShapeDtypeStruct((K, K), F32)),
        in_specs=[vmem] * 4,
        out_specs=(vmem, vmem),
        scratch_shapes=scratch,
        compiler_params=pltpu.CompilerParams(
            collective_id=0, has_side_effects=True, vmem_limit_bytes=56 * 2**20
        ),
        name="sweeps",
    )(sketch, inv_diag, upper, lower)


def solution(mesh):
    placed = (P("chain", None, None),) * 4
    return jax.shard_map(
        on_device,
        mesh=mesh,
        in_specs=placed,
        out_specs=(P("chain", None, None), P()),
        check_vma=False,
    )
```

time: 681 us -> 89.2 us (0.13)
  the two profiles are of different devices: /device:TPU:1 before, /device:TPU:0 now
where the time goes in v1:
time: 89.2 us; the launch traced here: 89.1 us
  Pallas kernels  86.2 us (97%)
  local copies, waits for them, and re-layouts  2.19 us (2%)
    pallas_call x1, Pallas kernels, on_device(): pl.pallas_call(kernel, out_shape=(jax.ShapeDtypeStruct((2, K, W), F32), j...  86.2 us
    unnamed x4, local copies, waits for them, and re-layouts  2.19 us

profile of v1, /device:TPU:0, one launch (start us, length us, event | category | flops | bytes accessed | tf_op | source)
XLA Modules:
  0.0 89.1 jit_solution(12554613570269368429)
XLA Ops:
  0.6 86.2 %sweeps.1 = (f32[2,64,256]{2,1,0:T(8,128)}, f32[64,64]{1,0:T(8,128)}) custom-call(f32[2,64,256]{2,1,0:T(8,128)} %sketch.1, f32[2,256,256]{2,1,0:T(8,128)} %inv_diag.1, f32[2,256,256]{2,1,0:T(8,128)} %upper.1, f32[2,256,256]{2,1,0:T(8,128)} %lower.1), custom_call_target="tpu_custom_call" | custom-call | tf_op jit(solution)/shard_map/sweeps/pallas_call | solution.py:359
  86.9 0.0 copy-start
  86.9 1.6 %copy.8 = f32[2,64,256]{2,1,0:T(8,128)} copy(f32[2,64,256]{2,1,0:T(8,128)} %get-tuple-element.4) | data formatting | bytes 262144
  88.5 0.0 copy-done
  88.5 0.6 copy.9
Async XLA Ops:
  86.9 1.6 %copy-start = (f32[64,64]{1,0:T(8,128)S(1)}, f32[64,64]{1,0:T(8,128)}, u32[]{:S(2)}) copy-start(f32[64,64]{1,0:T(8,128)} %get-tuple-element.5) | copy-start | bytes 49156

commit v2 on v1

v2 whole, which is shorter than its diff:
```python
import jax
import jax.numpy as jnp
from jax import lax
from jax.experimental import pallas as pl
from jax.experimental.pallas import tpu as pltpu
from jax.sharding import PartitionSpec as P

HIGH = lax.Precision.HIGHEST
MESH = pl.DeviceIdType.MESH
F32 = jnp.float32

W = 256
K = 64
HALF_M = 128
HALF_C = 32
HALF = HALF_M + HALF_C
ROWS = 2 * HALF
SEMS = 96


def dot(a, b):
    return jnp.dot(a, b, precision=HIGH, preferred_element_type=F32)


def mat(n):
    return jnp.concatenate([n[0:HALF_M], n[HALF : HALF + HALF_M]], axis=0)


def vec(n):
    return jnp.concatenate([n[HALF_M:HALF], n[HALF + HALF_M : ROWS]], axis=0)


def pack(m, c):
    return jnp.concatenate([m[0:HALF_M], c[0:HALF_C], m[HALF_M:W], c[HALF_C:K]], axis=0)


def add_vec(r, n):
    return jnp.concatenate(
        [
            r[0:HALF_M],
            r[HALF_M:HALF] + n[HALF_M:HALF],
            r[HALF : HALF + HALF_M],
            r[HALF + HALF_M : ROWS] + n[HALF + HALF_M : ROWS],
        ],
        axis=0,
    )


def compose(f, n):
    return add_vec(dot(f, mat(n)), n)


def apply(v, n):
    return dot(v, mat(n)) + vec(n)


def identity(rows, columns):
    return (
        lax.broadcasted_iota(jnp.int32, (rows, columns), 0) == lax.broadcasted_iota(jnp.int32, (rows, columns), 1)
    ).astype(F32)


def factor(gram):
    work = jnp.concatenate([gram, identity(K, K)], axis=1)
    count = K // 8
    blocks = [work[8 * b : 8 * b + 8] for b in range(count)]
    sub = lax.broadcasted_iota(jnp.int32, (8, 2 * K), 0)

    def wide(v):
        return jnp.broadcast_to(v, (8, 2 * K))

    out = []
    for b in range(count):
        columns = [{i: wide(blocks[i][:, 8 * b + j : 8 * b + j + 1]) for i in range(b, count)} for j in range(8)]
        corner = {(i, j): wide(columns[j][b][i : i + 1]) for j in range(8) for i in range(j, 8)}
        rows = [wide(blocks[b][j : j + 1]) for j in range(8)]
        scaled = []
        done = jnp.zeros((8, 2 * K), F32)
        pivots = jnp.ones((8, 2 * K), F32)
        for j in range(8):
            inverse = 1.0 / corner[j, j]
            scaled.append(rows[j] * inverse)
            pivots = jnp.where(sub == j, corner[j, j], pivots)
            done = jnp.where(sub == j, rows[j], done)
            for i in range(j + 1, 8):
                ratio = corner[i, j] * inverse
                rows[i] = rows[i] - ratio * rows[j]
                for n in range(i, 8):
                    corner[n, i] = corner[n, i] - corner[n, j] * ratio
                for n in range(b + 1, count):
                    columns[i][n] = columns[i][n] - columns[j][n] * ratio
        for i in range(b + 1, count):
            for j in range(8):
                blocks[i] = blocks[i] - columns[j][i] * scaled[j]
        out.append(done * lax.rsqrt(pivots))
    out = jnp.concatenate(out, axis=0)
    upper = jnp.where(
        lax.broadcasted_iota(jnp.int32, (K, K), 0) <= lax.broadcasted_iota(jnp.int32, (K, K), 1), out[:, 0:K], 0.0
    )
    return upper, out[:, K : 2 * K]


def kernel(
    sketch_in, inv_diag_in, upper_in, lower_in, basis, r_factor,
    sketch, inv_diag, upper, lower, own0, fc, gc, hc, y0s, y1s, dev_g, dev_h,
    xf, xg, xh, xpre, xsuf_h, xsuf_g, yf, yg, ypre, ysuf_g, row_h,
    zf, zc_in, zm_in, va, va_in, zg, entry, er, ep, ysuf_e, ends, tops, gown, gin, gx, gyz, gtot,
    send, recv, load,
):
    me = lax.axis_index("chain")
    c = lax.rem(me, 2)
    x = lax.rem(me // 2, 4)
    y = lax.rem(me // 8, 4)
    z = me // 32

    loads = []
    for src, dst in ((inv_diag_in, inv_diag), (upper_in, upper), (lower_in, lower)):
        for i in (0, 1):
            loads.append(pltpu.make_async_copy(src.at[i], dst.at[i], load.at[len(loads)]))
    loads.append(pltpu.make_async_copy(sketch_in, sketch, load.at[6]))
    for i in (0, 2, 6, 1, 3, 4, 5):
        loads[i].start()

    def at(zz, yy, xx, cc):
        return ((zz * 4 + yy) * 4 + xx) * 2 + cc

    def turn(place, k):
        return lax.rem(place + k, 4)

    sibling = at(z, y, x, 1 - c)
    xs = [at(z, y, turn(x, k), c) for k in range(4)]
    across = {(k, n): at(turn(z, k), turn(y, n), x, c) for k in (0, 1, 3, 2) for n in (0, 1, 3, 2) if (k, n) != (0, 0)}
    ys = [None, *(across[0, n] for n in (1, 2, 3))]
    zs = [None, *(across[k, 0] for k in (1, 2, 3))]

    barrier = pltpu.get_barrier_semaphore()
    for other in (sibling, *xs[1:], *across.values()):
        pl.semaphore_signal(barrier, inc=1, device_id=(other,), device_id_type=MESH)

    sent = []
    used = [0]

    def slot():
        used[0] += 1
        assert used[0] <= SEMS
        return used[0] - 1

    def start(src, dst, i, other):
        copy = pltpu.make_async_remote_copy(
            src_ref=src, dst_ref=dst, send_sem=send.at[i], recv_sem=recv.at[i], device_id=(other,), device_id_type=MESH
        )
        copy.start()
        sent.append(copy)

    def arrived(dst, i):
        pltpu.make_async_remote_copy(
            src_ref=dst, dst_ref=dst, send_sem=send.at[i], recv_sem=recv.at[i], device_id=(sibling,), device_id_type=MESH
        ).wait_recv()

    def drain(count):
        for copy in sent[:count]:
            copy.wait_send()
        del sent[:count]

    def rows_of(which, rows):
        return pl.ds(pl.multiple_of(which * rows, 8), rows)

    mine, others = rows_of(c, HALF), rows_of(1 - c, HALF)
    my_vec = pl.ds(pl.multiple_of(c * HALF + HALF_M, 8), HALF_C)

    def compose_half(f, n, which):
        r = dot(f, mat(n[...]))
        return jnp.concatenate(
            [r[0:HALF_M], r[HALF_M:HALF] + n[pl.ds(pl.multiple_of(which * HALF + HALF_M, 8), HALF_C)]], axis=0
        )

    class Gather:
        def __init__(self, ref, rows, place, peers, steps):
            self.ref, self.rows, self.place, self.peers, self.steps = ref, rows, place, peers, steps
            self.first = {k: slot() for k in steps}
            self.second = {k: slot() for k in steps}

        def part(self, k, which):
            return self.ref.at[turn(self.place, 4 - k), rows_of(which, self.rows)]

        def start(self):
            for k in self.steps:
                start(self.part(0, c), self.part(0, c), self.first[k], self.peers[k])

        def forward(self, between=None):
            for k in self.steps:
                arrived(self.part(k, c), self.first[k])
                start(self.part(k, c), self.part(k, c), self.second[k], sibling)
                if between is not None and k == self.steps[0]:
                    between()

        def finish(self):
            for k in self.steps:
                arrived(self.part(k, 1 - c), self.second[k])

    class Share:
        def __init__(self, ref, place, peers):
            self.ref, self.place, self.peers = ref, place, peers
            self.sems = {k: slot() for k in (1, 3, 2)}

        def start(self):
            for k in (1, 3, 2):
                start(self.ref.at[self.place], self.ref.at[self.place], self.sems[k], self.peers[k])

        def finish(self):
            for k in (1, 3, 2):
                arrived(self.ref.at[turn(self.place, 4 - k)], self.sems[k])

    def swap(ref, i):
        start(ref.at[c], ref.at[c], i, sibling)

    for i in (0, 2, 6):
        loads[i].wait()
    y0s[...] = dot(pack(-upper[0], sketch[0]), inv_diag[0])
    for i in (1, 3):
        loads[i].wait()
    own0[...] = dot(pack(-upper[1], sketch[1]), inv_diag[1])
    y1s[...] = compose(y0s[...], own0[...])
    fc[c] = y1s[...]
    pl.semaphore_wait(barrier, 1 + 3 + 15)
    sem_f, sem_g, sem_h = slot(), slot(), slot()
    swap(fc, sem_f)
    for i in (4, 5):
        loads[i].wait()
    gc[c] = dot(lower[1], lower[0])
    swap(gc, sem_g)
    arrived(fc.at[1 - c], sem_f)

    xf[x, mine] = compose_half(fc[0, mine], fc.at[1], c)
    gather_xf = Gather(xf, HALF, x, xs, (1, 3, 2))
    gather_xf.start()
    xf[x, others] = compose_half(fc[0, others], fc.at[1], 1 - c)

    hc[c] = dot(y0s[...] - dot(y1s[...], lower[1]), lower[0])
    swap(hc, sem_h)
    arrived(gc.at[1 - c], sem_g)
    xg[x] = dot(gc[1], gc[0])
    arrived(hc.at[1 - c], sem_h)
    late = compose(fc[0], hc[1])
    xh[x] = dot(late, gc[0]) + hc[0]
    second = c == 1
    eye = identity(W, W)
    dev_g[...] = jnp.where(second, eye, gc[1])
    dev_h[...] = jnp.where(second, 0.0, late)
    y0s[...] = jnp.where(second, compose(fc[0], y0s[...]), y0s[...])
    y1s[...] = jnp.where(second, xf[x], y1s[...])
    drain(3)

    gather_xg = Gather(xg, HALF_M, x, xs, (1, 3, 2))
    gather_xf.forward(gather_xg.start)
    gather_xf.finish()
    q23 = compose(xf[2], xf[3])
    xsuf_h[0] = q23
    xpre[2, mine] = compose_half(xf[0, mine], xf.at[1], c)
    yf[y, mine] = compose_half(xpre[2, mine], xsuf_h.at[0], c)

    gather_yf = Gather(yf, HALF, y, ys, (1, 3, 2))
    gather_yf.start()
    xpre[2, others] = compose_half(xf[0, others], xf.at[1], 1 - c)
    yf[y, others] = compose_half(xpre[2, others], xsuf_h.at[0], 1 - c)
    xpre[0] = pack(eye, jnp.zeros((K, W), F32))
    xpre[1] = xf[0]
    xpre[3] = compose(xpre[2], xf[2])
    y0s[...] = compose(xpre[x], y0s[...])
    y1s[...] = compose(xpre[x], y1s[...])
    dev_h[...] = compose(xpre[x], dev_h[...])
    drain(9)

    gather_xh = Gather(xh, HALF, x, xs, (1, 3, 2))
    gather_yf.forward(gather_xh.start)
    gather_xg.forward()
    gather_yf.finish()
    q23 = compose(yf[2], yf[3])
    ypre[2] = compose(yf[0], yf[1])
    zf[...] = compose(ypre[2], q23)

    sem_c, sem_m, sem_m2, sem_v1, sem_v2 = slot(), slot(), slot(), slot(), slot()
    start(zf.at[my_vec], zc_in, sem_c, zs[1])
    my_m = pl.ds(pl.multiple_of(c * HALF, 8), HALF_M)
    my_half, other_half = rows_of(c, HALF_M), rows_of(1 - c, HALF_M)
    start(zf.at[my_m], zm_in.at[my_half], sem_m, zs[1])

    gather_xg.finish()
    xsuf_g[3] = eye
    xsuf_g[2] = xg[3]
    xsuf_g[1] = dot(xg[3], xg[2])
    xsuf_g[0] = dot(xsuf_g[1], xg[1])
    yg[y] = dot(xsuf_g[0], xg[0])
    gather_yg = Gather(yg, HALF_M, y, ys, (1, 3, 2))
    gather_yg.start()
    ypre[0] = pack(eye, jnp.zeros((K, W), F32))
    ypre[1] = yf[0]

    arrived(zc_in, sem_c)
    plane_m = mat(zf[...])
    va[...] = dot(zc_in[...], plane_m) + zf[my_vec]
    start(va, va_in.at[0], sem_v1, zs[1])
    start(va, va_in.at[1], sem_v2, zs[2])
    arrived(zm_in.at[my_half], sem_m)
    start(zm_in.at[my_half], zm_in.at[my_half], sem_m2, sibling)

    gather_xh.forward()
    ypre[3] = compose(ypre[2], yf[2])
    gather_xh.finish()
    xsuf_h[3] = jnp.zeros((ROWS, W), F32)
    xsuf_h[2] = compose(xpre[3], xh[3])
    xsuf_h[1] = dot(xsuf_h[2], xg[2]) + compose(xpre[2], xh[2])
    xsuf_h[0] = dot(xsuf_h[1], xg[1]) + compose(xf[0], xh[1])
    row_h[...] = compose(ypre[y], dot(xsuf_h[0], xg[0]) + xh[0])
    drain(18)

    arrived(zm_in.at[other_half], sem_m2)
    arrived(va_in.at[0], sem_v1)
    arrived(va_in.at[1], sem_v2)
    last = dot(va_in[1], zm_in[...]) + zc_in[...]
    start_row = jnp.where(z == 0, 0.0, jnp.where(z == 1, zc_in[...], jnp.where(z == 2, va_in[0], last)))

    er[y] = dot(start_row, mat(row_h[...])) + row_h[my_vec]
    share_er = Share(er, y, ys)
    share_er.start()
    entry[c] = start_row
    sem_entry = slot()
    swap(entry, sem_entry)

    dev_h[...] = dot(xsuf_h[x], dev_g[...]) + dev_h[...]
    dev_g[...] = dot(xsuf_g[x], dev_g[...])
    arrived(entry.at[1 - c], sem_entry)
    row = apply(jnp.concatenate([entry[0], entry[1]], axis=0), ypre[y])
    x1 = apply(row, y1s[...]) - apply(row, dev_h[...])
    x0 = apply(row, y0s[...]) - dot(x1, lower[1])

    gather_yg.forward()
    gather_yg.finish()
    ysuf_g[3] = eye
    ysuf_g[2] = yg[3]
    ysuf_g[1] = dot(yg[3], yg[2])
    ysuf_g[0] = dot(ysuf_g[1], yg[1])
    zg[z] = dot(ysuf_g[0], yg[0])
    gather_zg = Gather(zg, HALF_M, z, zs, (3, 2))
    gather_zg.start()

    share_er.finish()
    ysuf_e[3] = jnp.zeros((HALF_C, W), F32)
    ysuf_e[2] = er[3]
    ysuf_e[1] = dot(er[3], yg[2]) + er[2]
    ysuf_e[0] = dot(ysuf_e[1], yg[1]) + er[1]
    ep[z] = dot(ysuf_e[0], yg[0]) + er[0]

    share_ep = Share(ep, z, zs)
    share_ep.start()
    ends[c] = ysuf_e[y]
    sem_ends = slot()
    swap(ends, sem_ends)
    to_w1 = dot(ysuf_g[y], dev_g[...])
    to_w0 = dot(to_w1, lower[1])
    arrived(ends.at[1 - c], sem_ends)
    from_row = dot(jnp.concatenate([ends[0], ends[1]], axis=0), dev_g[...])
    x1 = x1 - from_row
    x0 = x0 + dot(from_row, lower[1])
    drain(23)
    gather_zg.forward()
    gather_zg.finish()
    share_ep.finish()
    two = dot(ep[3], zg[2]) + ep[2]
    three = dot(two, zg[1]) + ep[1]
    tops[c] = jnp.where(z == 3, 0.0, jnp.where(z == 2, ep[3], jnp.where(z == 1, two, three)))
    sem_tops = slot()
    swap(tops, sem_tops)
    arrived(tops.at[1 - c], sem_tops)
    top = jnp.concatenate([tops[0], tops[1]], axis=0)
    x1 = x1 - dot(top, to_w1)
    x0 = x0 + dot(top, to_w0)

    both = jnp.concatenate([x0, x1], axis=1)
    gram = lax.dot_general(both, both, (((1,), (1,)), ((), ())), precision=HIGH, preferred_element_type=F32)
    gram = jnp.concatenate([gram[0 : K // 2], gram[K // 2 : K]], axis=1)
    gown[0] = gram[0 : K // 4]
    gown[1] = gram[K // 4 : K // 2]
    sem_gin, sem_gtot = slot(), slot()
    start(gown.at[1 - c], gin, sem_gin, sibling)
    arrived(gin, sem_gin)
    gx[x] = gown[c] + gin[...]
    share_gx = Share(gx, x, xs)
    share_gx.start()
    drain(9)
    share_gx.finish()
    own = z * 4 + y
    gyz[own] = (gx[0] + gx[1]) + (gx[2] + gx[3])
    sems = {step: slot() for step in across}
    for step, other in across.items():
        start(gyz.at[own], gyz.at[own], sems[step], other)
    drain(3)
    for (k, n), i in sems.items():
        arrived(gyz.at[turn(z, 4 - k) * 4 + turn(y, 4 - n)], i)
    terms = [gyz[i] for i in range(16)]
    while len(terms) > 1:
        terms = [terms[i] + terms[i + 1] for i in range(0, len(terms), 2)]
    gtot[c] = terms[0]
    swap(gtot, sem_gtot)
    drain(15)
    arrived(gtot.at[1 - c], sem_gtot)
    total = jnp.concatenate([gtot[0], gtot[1]], axis=0) / (256 * W)
    r, inverse = factor(jnp.concatenate([total[:, 0:K], total[:, K : 2 * K]], axis=0))
    r_factor[...] = r
    basis[0] = dot(inverse, x0)
    basis[1] = dot(inverse, x1)
    drain(len(sent))


def on_device(sketch, inv_diag, upper, lower):
    def buf(*shape):
        return pltpu.VMEM(shape, F32)

    affine = (ROWS, W)
    part = (HALF_C, W)
    quarter = (K // 4, 2 * K)
    vmem = pl.BlockSpec(memory_space=pltpu.VMEM)
    scratch = [
        buf(2, K, W), buf(2, W, W), buf(2, W, W), buf(2, W, W), buf(*affine), buf(2, *affine), buf(2, W, W), buf(2, *affine),
        buf(*affine), buf(*affine), buf(W, W), buf(*affine),
        buf(4, *affine), buf(4, W, W), buf(4, *affine), buf(4, *affine), buf(4, *affine), buf(4, W, W),
        buf(4, *affine), buf(4, W, W), buf(4, *affine), buf(4, W, W), buf(*affine),
        buf(*affine), buf(*part), buf(W, W), buf(*part), buf(2, *part), buf(4, W, W), buf(2, *part),
        buf(4, *part), buf(4, *part), buf(4, *part), buf(2, *part), buf(2, *part),
        buf(2, *quarter), buf(*quarter), buf(4, *quarter), buf(16, *quarter), buf(2, *quarter),
        pltpu.SemaphoreType.DMA((SEMS,)), pltpu.SemaphoreType.DMA((SEMS,)), pltpu.SemaphoreType.DMA((7,)),
    ]
    return pl.pallas_call(
        kernel,
        out_shape=(jax.ShapeDtypeStruct((2, K, W), F32), jax.ShapeDtypeStruct((K, K), F32)),
        in_specs=[pl.BlockSpec(memory_space=pl.ANY)] * 4,
        out_specs=(vmem, vmem),
        scratch_shapes=scratch,
        compiler_params=pltpu.CompilerParams(
            collective_id=0, has_side_effects=True, vmem_limit_bytes=56 * 2**20
        ),
        name="sweeps",
    )(sketch, inv_diag, upper, lower)


def solution(mesh):
    placed = (P("chain", None, None),) * 4
    return jax.shard_map(
        on_device,
        mesh=mesh,
        in_specs=placed,
        out_specs=(P("chain", None, None), P()),
        check_vma=False,
    )
```

time: 89.2 us -> 81 us (0.908)
  the two profiles are of different devices: /device:TPU:0 before, /device:TPU:1 now
where the time goes in v2:
time: 81 us; the launch traced here: 80.8 us
  Pallas kernels  78 us (96%)
  local copies, waits for them, and re-layouts  2.19 us (3%)
    pallas_call x1, Pallas kernels, on_device(): pl.pallas_call(kernel, out_shape=(jax.ShapeDtypeStruct((2, K, W), F32), j...  78 us
    unnamed x4, local copies, waits for them, and re-layouts  2.19 us

profile of v2, /device:TPU:1, one launch (start us, length us, event | category | flops | bytes accessed | tf_op | source)
XLA Modules:
  0.0 80.8 jit_solution(9770248790631875639)
XLA Ops:
  0.6 78.0 %sweeps.1 = (f32[2,64,256]{2,1,0:T(8,128)}, f32[64,64]{1,0:T(8,128)}) custom-call(f32[2,64,256]{2,1,0:T(8,128)} %sketch_in.1, f32[2,256,256]{2,1,0:T(8,128)} %inv_diag_in.1, f32[2,256,256]{2,1,0:T(8,128)} %upper_in.1, f32[2,256,256]{2,1,0:T(8,128)} %lower_in.1), custom_call_target="tpu_custom_call" | custom-call | tf_op jit(solution)/shard_map/sweeps/pallas_call | solution.py:433
  78.6 0.0 copy-start
  78.6 1.6 %copy.8 = f32[2,64,256]{2,1,0:T(8,128)} copy(f32[2,64,256]{2,1,0:T(8,128)} %get-tuple-element.4) | data formatting | bytes 262144
  80.2 0.0 copy-done
  80.2 0.6 copy.9
Async XLA Ops:
  78.6 1.6 %copy-start = (f32[64,64]{1,0:T(8,128)S(1)}, f32[64,64]{1,0:T(8,128)}, u32[]{:S(2)}) copy-start(f32[64,64]{1,0:T(8,128)} %get-tuple-element.5) | copy-start | bytes 49156

commit v3 on v2

--- a/solution.py
+++ b/solution.py
@@ -15,7 +15,7 @@
 HALF_C = 32
 HALF = HALF_M + HALF_C
 ROWS = 2 * HALF
-SEMS = 96
+SEMS = 128
 
 
 def dot(a, b):
@@ -198,6 +198,41 @@
             for k in self.steps:
                 arrived(self.part(k, 1 - c), self.second[k])
 
+    class Relay:
+        cut = HALF // 2
+
+        def __init__(self, ref, place, peers):
+            self.ref, self.place, self.peers = ref, place, peers
+            self.first = {(k, p): slot() for k in (1, 3, 2) for p in (0, 1)}
+            self.second = {(k, p): slot() for k in (1, 3, 2) for p in (0, 1)}
+
+        def part(self, k, p, which):
+            at_row = pl.multiple_of(which * HALF + p * self.cut, 8)
+            return self.ref.at[turn(self.place, 4 - k), pl.ds(at_row, self.cut)]
+
+        def start(self):
+            for k, p in ((1, 0), (3, 1), (1, 1), (3, 0)):
+                start(self.part(0, p, c), self.part(0, p, c), self.first[k, p], self.peers[k])
+
+        def inside(self, k, p):
+            start(self.part(k, p, c), self.part(k, p, c), self.second[k, p], sibling)
+
+        def relay(self):
+            for k, p in ((1, 0), (3, 1)):
+                arrived(self.part(k, p, c), self.first[k, p])
+                start(self.part(k, p, c), self.part(k, p, c), self.first[2, p], self.peers[k])
+            for k, p in ((1, 0), (3, 1)):
+                self.inside(k, p)
+
+        def forward(self):
+            for k, p in ((1, 1), (3, 0), (2, 0), (2, 1)):
+                arrived(self.part(k, p, c), self.first[k, p])
+                self.inside(k, p)
+
+        def finish(self):
+            for k, p in self.second:
+                arrived(self.part(k, p, 1 - c), self.second[k, p])
+
     class Share:
         def __init__(self, ref, place, peers):
             self.ref, self.place, self.peers = ref, place, peers
@@ -232,14 +267,17 @@
     arrived(fc.at[1 - c], sem_f)
 
     xf[x, mine] = compose_half(fc[0, mine], fc.at[1], c)
-    gather_xf = Gather(xf, HALF, x, xs, (1, 3, 2))
+    gather_xf = Relay(xf, x, xs)
     gather_xf.start()
     xf[x, others] = compose_half(fc[0, others], fc.at[1], 1 - c)
-
     hc[c] = dot(y0s[...] - dot(y1s[...], lower[1]), lower[0])
     swap(hc, sem_h)
     arrived(gc.at[1 - c], sem_g)
     xg[x] = dot(gc[1], gc[0])
+    gather_xf.relay()
+
+    gather_xg = Gather(xg, HALF_M, x, xs, (1, 3, 2))
+    gather_xg.start()
     arrived(hc.at[1 - c], sem_h)
     late = compose(fc[0], hc[1])
     xh[x] = dot(late, gc[0]) + hc[0]
@@ -250,17 +288,17 @@
     y0s[...] = jnp.where(second, compose(fc[0], y0s[...]), y0s[...])
     y1s[...] = jnp.where(second, xf[x], y1s[...])
     drain(3)
-
-    gather_xg = Gather(xg, HALF_M, x, xs, (1, 3, 2))
-    gather_xf.forward(gather_xg.start)
+    gather_xf.forward()
     gather_xf.finish()
     q23 = compose(xf[2], xf[3])
     xsuf_h[0] = q23
     xpre[2, mine] = compose_half(xf[0, mine], xf.at[1], c)
     yf[y, mine] = compose_half(xpre[2, mine], xsuf_h.at[0], c)
 
-    gather_yf = Gather(yf, HALF, y, ys, (1, 3, 2))
+    gather_yf = Relay(yf, y, ys)
     gather_yf.start()
+    gather_xh = Gather(xh, HALF, x, xs, (1, 3, 2))
+    gather_xh.start()
     xpre[2, others] = compose_half(xf[0, others], xf.at[1], 1 - c)
     yf[y, others] = compose_half(xpre[2, others], xsuf_h.at[0], 1 - c)
     xpre[0] = pack(eye, jnp.zeros((K, W), F32))
@@ -268,23 +306,11 @@
     xpre[3] = compose(xpre[2], xf[2])
     y0s[...] = compose(xpre[x], y0s[...])
     y1s[...] = compose(xpre[x], y1s[...])
+    drain(12)
+    gather_yf.relay()
+
+    gather_xg.forward()
     dev_h[...] = compose(xpre[x], dev_h[...])
-    drain(9)
-
-    gather_xh = Gather(xh, HALF, x, xs, (1, 3, 2))
-    gather_yf.forward(gather_xh.start)
-    gather_xg.forward()
-    gather_yf.finish()
-    q23 = compose(yf[2], yf[3])
-    ypre[2] = compose(yf[0], yf[1])
-    zf[...] = compose(ypre[2], q23)
-
-    sem_c, sem_m, sem_m2, sem_v1, sem_v2 = slot(), slot(), slot(), slot(), slot()
-    start(zf.at[my_vec], zc_in, sem_c, zs[1])
-    my_m = pl.ds(pl.multiple_of(c * HALF, 8), HALF_M)
-    my_half, other_half = rows_of(c, HALF_M), rows_of(1 - c, HALF_M)
-    start(zf.at[my_m], zm_in.at[my_half], sem_m, zs[1])
-
     gather_xg.finish()
     xsuf_g[3] = eye
     xsuf_g[2] = xg[3]
@@ -293,26 +319,41 @@
     yg[y] = dot(xsuf_g[0], xg[0])
     gather_yg = Gather(yg, HALF_M, y, ys, (1, 3, 2))
     gather_yg.start()
+    gather_yf.forward()
+    gather_yf.finish()
+    q23 = compose(yf[2], yf[3])
+    xsuf_h[0] = q23
+    ypre[2, mine] = compose_half(yf[0, mine], yf.at[1], c)
+    zf[my_vec] = dot(ypre[2, my_vec], mat(q23)) + xsuf_h[0, my_vec]
+
+    sem_c, sem_m, sem_m2, sem_v1, sem_v2 = slot(), slot(), slot(), slot(), slot()
+    start(zf.at[my_vec], zc_in, sem_c, zs[1])
+    my_m = pl.ds(pl.multiple_of(c * HALF, 8), HALF_M)
+    other_m = pl.ds(pl.multiple_of((1 - c) * HALF, 8), HALF_M)
+    my_half, other_half = rows_of(c, HALF_M), rows_of(1 - c, HALF_M)
+    zf[my_m] = dot(ypre[2, my_m], mat(q23))
+    start(zf.at[my_m], zm_in.at[my_half], sem_m, zs[1])
+    ypre[2, others] = compose_half(yf[0, others], yf.at[1], 1 - c)
+    zf[other_m] = dot(ypre[2, other_m], mat(q23))
+    gather_xh.forward()
     ypre[0] = pack(eye, jnp.zeros((K, W), F32))
     ypre[1] = yf[0]
+    gather_xh.finish()
+    xsuf_h[3] = jnp.zeros((ROWS, W), F32)
+    xsuf_h[2] = compose(xpre[3], xh[3])
 
     arrived(zc_in, sem_c)
-    plane_m = mat(zf[...])
-    va[...] = dot(zc_in[...], plane_m) + zf[my_vec]
+    va[...] = dot(zc_in[...], mat(zf[...])) + zf[my_vec]
     start(va, va_in.at[0], sem_v1, zs[1])
     start(va, va_in.at[1], sem_v2, zs[2])
     arrived(zm_in.at[my_half], sem_m)
     start(zm_in.at[my_half], zm_in.at[my_half], sem_m2, sibling)
 
-    gather_xh.forward()
-    ypre[3] = compose(ypre[2], yf[2])
-    gather_xh.finish()
-    xsuf_h[3] = jnp.zeros((ROWS, W), F32)
-    xsuf_h[2] = compose(xpre[3], xh[3])
     xsuf_h[1] = dot(xsuf_h[2], xg[2]) + compose(xpre[2], xh[2])
     xsuf_h[0] = dot(xsuf_h[1], xg[1]) + compose(xf[0], xh[1])
+    ypre[3] = compose(ypre[2], yf[2])
     row_h[...] = compose(ypre[y], dot(xsuf_h[0], xg[0]) + xh[0])
-    drain(18)
+    drain(24)
 
     arrived(zm_in.at[other_half], sem_m2)
     arrived(va_in.at[0], sem_v1)
@@ -326,13 +367,6 @@
     entry[c] = start_row
     sem_entry = slot()
     swap(entry, sem_entry)
-
-    dev_h[...] = dot(xsuf_h[x], dev_g[...]) + dev_h[...]
-    dev_g[...] = dot(xsuf_g[x], dev_g[...])
-    arrived(entry.at[1 - c], sem_entry)
-    row = apply(jnp.concatenate([entry[0], entry[1]], axis=0), ypre[y])
-    x1 = apply(row, y1s[...]) - apply(row, dev_h[...])
-    x0 = apply(row, y0s[...]) - dot(x1, lower[1])
 
     gather_yg.forward()
     gather_yg.finish()
@@ -343,6 +377,13 @@
     zg[z] = dot(ysuf_g[0], yg[0])
     gather_zg = Gather(zg, HALF_M, z, zs, (3, 2))
     gather_zg.start()
+
+    dev_h[...] = dot(xsuf_h[x], dev_g[...]) + dev_h[...]
+    dev_g[...] = dot(xsuf_g[x], dev_g[...])
+    arrived(entry.at[1 - c], sem_entry)
+    row = apply(jnp.concatenate([entry[0], entry[1]], axis=0), ypre[y])
+    x1 = apply(row, y1s[...]) - apply(row, dev_h[...])
+    x0 = apply(row, y0s[...]) - dot(x1, lower[1])
 
     share_er.finish()
     ysuf_e[3] = jnp.zeros((HALF_C, W), F32)

time: 81 us -> 75.1 us (0.927)
  Pallas kernels: 78 us -> 72.1 us
    pallas_call x1, Pallas kernels: 78 us -> 72.1 us  [on_device(): pl.pallas_call(kernel, out_shape=(jax.ShapeDtypeStruct((2, K, W), F32), j...]
where the time goes in v3:
time: 75.1 us; the launch traced here: 74.9 us
  Pallas kernels  72.1 us (96%)
  local copies, waits for them, and re-layouts  2.19 us (3%)
    pallas_call x1, Pallas kernels, on_device(): pl.pallas_call(kernel, out_shape=(jax.ShapeDtypeStruct((2, K, W), F32), j...  72.1 us
    unnamed x4, local copies, waits for them, and re-layouts  2.19 us

profile of v3, /device:TPU:1, one launch (start us, length us, event | category | flops | bytes accessed | tf_op | source)
XLA Modules:
  0.0 74.9 jit_solution(17817467086587814411)
XLA Ops:
  0.6 72.1 %sweeps.1 = (f32[2,64,256]{2,1,0:T(8,128)}, f32[64,64]{1,0:T(8,128)}) custom-call(f32[2,64,256]{2,1,0:T(8,128)} %sketch_in.1, f32[2,256,256]{2,1,0:T(8,128)} %inv_diag_in.1, f32[2,256,256]{2,1,0:T(8,128)} %upper_in.1, f32[2,256,256]{2,1,0:T(8,128)} %lower_in.1), custom_call_target="tpu_custom_call" | custom-call | tf_op jit(solution)/shard_map/sweeps/pallas_call | solution.py:474
  72.7 0.0 copy-start
  72.7 1.6 %copy.8 = f32[2,64,256]{2,1,0:T(8,128)} copy(f32[2,64,256]{2,1,0:T(8,128)} %get-tuple-element.4) | data formatting | bytes 262144
  74.3 0.0 copy-done
  74.3 0.6 copy.9
Async XLA Ops:
  72.7 1.6 %copy-start = (f32[64,64]{1,0:T(8,128)S(1)}, f32[64,64]{1,0:T(8,128)}, u32[]{:S(2)}) copy-start(f32[64,64]{1,0:T(8,128)} %get-tuple-element.5) | copy-start | bytes 49156

commit v4 on v3

--- a/solution.py
+++ b/solution.py
@@ -103,7 +103,7 @@
 def kernel(
     sketch_in, inv_diag_in, upper_in, lower_in, basis, r_factor,
     sketch, inv_diag, upper, lower, own0, fc, gc, hc, y0s, y1s, dev_g, dev_h,
-    xf, xg, xh, xpre, xsuf_h, xsuf_g, yf, yg, ypre, ysuf_g, row_h,
+    xf, xg, xh, xpre, xsuf_h, xsuf_g, yf, yg, ypre, ysuf_g, ysum, row_h,
     zf, zc_in, zm_in, va, va_in, zg, entry, er, ep, ysuf_e, ends, tops, gown, gin, gx, gyz, gtot,
     send, recv, load,
 ):
@@ -145,21 +145,28 @@
         assert used[0] <= SEMS
         return used[0] - 1
 
-    def start(src, dst, i, other):
+    def on(condition, act):
+        if condition is None:
+            act()
+        else:
+            pl.when(condition)(act)
+
+    def start(src, dst, i, other, condition=None):
         copy = pltpu.make_async_remote_copy(
             src_ref=src, dst_ref=dst, send_sem=send.at[i], recv_sem=recv.at[i], device_id=(other,), device_id_type=MESH
         )
-        copy.start()
-        sent.append(copy)
-
-    def arrived(dst, i):
-        pltpu.make_async_remote_copy(
+        on(condition, copy.start)
+        sent.append((condition, copy))
+
+    def arrived(dst, i, condition=None):
+        copy = pltpu.make_async_remote_copy(
             src_ref=dst, dst_ref=dst, send_sem=send.at[i], recv_sem=recv.at[i], device_id=(sibling,), device_id_type=MESH
-        ).wait_recv()
+        )
+        on(condition, copy.wait_recv)
 
     def drain(count):
-        for copy in sent[:count]:
-            copy.wait_send()
+        for condition, copy in sent[:count]:
+            on(condition, copy.wait_send)
         del sent[:count]
 
     def rows_of(which, rows):
@@ -175,8 +182,10 @@
         )
 
     class Gather:
-        def __init__(self, ref, rows, place, peers, steps):
+        def __init__(self, ref, rows, place, peers, steps, gives=None, takes=None):
             self.ref, self.rows, self.place, self.peers, self.steps = ref, rows, place, peers, steps
+            self.gives = dict(zip(steps, gives)) if gives else {}
+            self.takes = dict(zip(steps, takes)) if takes else {}
             self.first = {k: slot() for k in steps}
             self.second = {k: slot() for k in steps}
 
@@ -185,18 +194,16 @@
 
         def start(self):
             for k in self.steps:
-                start(self.part(0, c), self.part(0, c), self.first[k], self.peers[k])
-
-        def forward(self, between=None):
+                start(self.part(0, c), self.part(0, c), self.first[k], self.peers[k], self.gives.get(k))
+
+        def forward(self):
             for k in self.steps:
-                arrived(self.part(k, c), self.first[k])
-                start(self.part(k, c), self.part(k, c), self.second[k], sibling)
-                if between is not None and k == self.steps[0]:
-                    between()
+                arrived(self.part(k, c), self.first[k], self.takes.get(k))
+                start(self.part(k, c), self.part(k, c), self.second[k], sibling, self.takes.get(k))
 
         def finish(self):
             for k in self.steps:
-                arrived(self.part(k, 1 - c), self.second[k])
+                arrived(self.part(k, 1 - c), self.second[k], self.takes.get(k))
 
     class Relay:
         cut = HALF // 2
@@ -341,6 +348,7 @@
     gather_xh.finish()
     xsuf_h[3] = jnp.zeros((ROWS, W), F32)
     xsuf_h[2] = compose(xpre[3], xh[3])
+    xsuf_h[1] = dot(xsuf_h[2], xg[2]) + compose(xpre[2], xh[2])
 
     arrived(zc_in, sem_c)
     va[...] = dot(zc_in[...], mat(zf[...])) + zf[my_vec]
@@ -349,9 +357,8 @@
     arrived(zm_in.at[my_half], sem_m)
     start(zm_in.at[my_half], zm_in.at[my_half], sem_m2, sibling)
 
-    xsuf_h[1] = dot(xsuf_h[2], xg[2]) + compose(xpre[2], xh[2])
+    ypre[3] = compose(ypre[2], yf[2])
     xsuf_h[0] = dot(xsuf_h[1], xg[1]) + compose(xf[0], xh[1])
-    ypre[3] = compose(ypre[2], yf[2])
     row_h[...] = compose(ypre[y], dot(xsuf_h[0], xg[0]) + xh[0])
     drain(24)
 
@@ -367,7 +374,6 @@
     entry[c] = start_row
     sem_entry = slot()
     swap(entry, sem_entry)
-
     gather_yg.forward()
     gather_yg.finish()
     ysuf_g[3] = eye
@@ -375,8 +381,12 @@
     ysuf_g[1] = dot(yg[3], yg[2])
     ysuf_g[0] = dot(ysuf_g[1], yg[1])
     zg[z] = dot(ysuf_g[0], yg[0])
-    gather_zg = Gather(zg, HALF_M, z, zs, (3, 2))
+    gather_zg = Gather(zg, HALF_M, z, zs, (3, 2), ((z == 1) | (z == 2), z == 2), (z < 2, z == 0))
     gather_zg.start()
+
+    ysum[0] = yg[0]
+    ysum[1] = dot(yg[1], yg[0])
+    ysum[2] = dot(yg[2], ysum[1])
 
     dev_h[...] = dot(xsuf_h[x], dev_g[...]) + dev_h[...]
     dev_g[...] = dot(xsuf_g[x], dev_g[...])
@@ -386,14 +396,14 @@
     x0 = apply(row, y0s[...]) - dot(x1, lower[1])
 
     share_er.finish()
+    ep[z] = dot(jnp.concatenate([er[1], er[2], er[3]], axis=1), ysum[...].reshape(3 * W, W)) + er[0]
+
+    share_ep = Share(ep, z, zs)
+    share_ep.start()
     ysuf_e[3] = jnp.zeros((HALF_C, W), F32)
     ysuf_e[2] = er[3]
     ysuf_e[1] = dot(er[3], yg[2]) + er[2]
     ysuf_e[0] = dot(ysuf_e[1], yg[1]) + er[1]
-    ep[z] = dot(ysuf_e[0], yg[0]) + er[0]
-
-    share_ep = Share(ep, z, zs)
-    share_ep.start()
     ends[c] = ysuf_e[y]
     sem_ends = slot()
     swap(ends, sem_ends)
@@ -465,7 +475,7 @@
         buf(2, K, W), buf(2, W, W), buf(2, W, W), buf(2, W, W), buf(*affine), buf(2, *affine), buf(2, W, W), buf(2, *affine),
         buf(*affine), buf(*affine), buf(W, W), buf(*affine),
         buf(4, *affine), buf(4, W, W), buf(4, *affine), buf(4, *affine), buf(4, *affine), buf(4, W, W),
-        buf(4, *affine), buf(4, W, W), buf(4, *affine), buf(4, W, W), buf(*affine),
+        buf(4, *affine), buf(4, W, W), buf(4, *affine), buf(4, W, W), buf(3, W, W), buf(*affine),
         buf(*affine), buf(*part), buf(W, W), buf(*part), buf(2, *part), buf(4, W, W), buf(2, *part),
         buf(4, *part), buf(4, *part), buf(4, *part), buf(2, *part), buf(2, *part),
         buf(2, *quarter), buf(*quarter), buf(4, *quarter), buf(16, *quarter), buf(2, *quarter),

time: 75.1 us -> 72.9 us (0.971)
  Pallas kernels: 72.1 us -> 69.9 us
    pallas_call x1, Pallas kernels: 72.1 us -> 69.9 us  [on_device(): pl.pallas_call(kernel, out_shape=(jax.ShapeDtypeStruct((2, K, W), F32), j...]
where the time goes in v4:
time: 72.9 us; the launch traced here: 72.8 us
  Pallas kernels  69.9 us (96%)
  local copies, waits for them, and re-layouts  2.19 us (3%)
    pallas_call x1, Pallas kernels, on_device(): pl.pallas_call(kernel, out_shape=(jax.ShapeDtypeStruct((2, K, W), F32), j...  69.9 us
    unnamed x4, local copies, waits for them, and re-layouts  2.19 us

profile of v4, /device:TPU:1, one launch (start us, length us, event | category | flops | bytes accessed | tf_op | source)
XLA Modules:
  0.0 72.8 jit_solution(6012638290619359418)
XLA Ops:
  0.6 69.9 %sweeps.1 = (f32[2,64,256]{2,1,0:T(8,128)}, f32[64,64]{1,0:T(8,128)}) custom-call(f32[2,64,256]{2,1,0:T(8,128)} %sketch_in.1, f32[2,256,256]{2,1,0:T(8,128)} %inv_diag_in.1, f32[2,256,256]{2,1,0:T(8,128)} %upper_in.1, f32[2,256,256]{2,1,0:T(8,128)} %lower_in.1), custom_call_target="tpu_custom_call" | custom-call | tf_op jit(solution)/shard_map/sweeps/pallas_call | solution.py:484
  70.6 0.0 copy-start
  70.6 1.6 %copy.8 = f32[2,64,256]{2,1,0:T(8,128)} copy(f32[2,64,256]{2,1,0:T(8,128)} %get-tuple-element.4) | data formatting | bytes 262144
  72.2 0.0 copy-done
  72.2 0.6 copy.9
Async XLA Ops:
  70.6 1.6 %copy-start = (f32[64,64]{1,0:T(8,128)S(1)}, f32[64,64]{1,0:T(8,128)}, u32[]{:S(2)}) copy-start(f32[64,64]{1,0:T(8,128)} %get-tuple-element.5) | copy-start | bytes 49156

commit v5 on v4

--- a/solution.py
+++ b/solution.py
@@ -15,7 +15,7 @@
 HALF_C = 32
 HALF = HALF_M + HALF_C
 ROWS = 2 * HALF
-SEMS = 128
+SEMS = 160
 
 
 def dot(a, b):
@@ -104,7 +104,7 @@
     sketch_in, inv_diag_in, upper_in, lower_in, basis, r_factor,
     sketch, inv_diag, upper, lower, own0, fc, gc, hc, y0s, y1s, dev_g, dev_h,
     xf, xg, xh, xpre, xsuf_h, xsuf_g, yf, yg, ypre, ysuf_g, ysum, row_h,
-    zf, zc_in, zm_in, va, va_in, zg, entry, er, ep, ysuf_e, ends, tops, gown, gin, gx, gyz, gtot,
+    zf, zc_in, zm_in, va, va_in, zg, entry, er, ep, ysuf_e, ends, tops, gown, gx, gyz, gtot,
     send, recv, load,
 ):
     me = lax.axis_index("chain")
@@ -134,7 +134,7 @@
     zs = [None, *(across[k, 0] for k in (1, 2, 3))]
 
     barrier = pltpu.get_barrier_semaphore()
-    for other in (sibling, *xs[1:], *across.values()):
+    for other in (sibling, *xs[1:], *(at(z, y, turn(x, k), 1 - c) for k in (1, 2, 3)), *across.values()):
         pl.semaphore_signal(barrier, inc=1, device_id=(other,), device_id_type=MESH)
 
     sent = []
@@ -206,39 +206,53 @@
                 arrived(self.part(k, 1 - c), self.second[k], self.takes.get(k))
 
     class Relay:
-        cut = HALF // 2
+        handed = ((1, 0), (3, 3), (1, 1), (3, 2))
+        piece = HALF // 4
 
         def __init__(self, ref, place, peers):
             self.ref, self.place, self.peers = ref, place, peers
-            self.first = {(k, p): slot() for k in (1, 3, 2) for p in (0, 1)}
-            self.second = {(k, p): slot() for k in (1, 3, 2) for p in (0, 1)}
-
-        def part(self, k, p, which):
-            at_row = pl.multiple_of(which * HALF + p * self.cut, 8)
-            return self.ref.at[turn(self.place, 4 - k), pl.ds(at_row, self.cut)]
+            self.first = {key: slot() for key in (*self.handed, (1, "rest"), (3, "rest"))}
+            self.far = {key: slot() for key in self.handed}
+            self.second = {key: slot() for key in ((1, 0), (3, 1), (1, 1), (3, 0), (2, None))}
+
+        def rows(self, k, low, count, which):
+            at_row = pl.multiple_of(which * HALF + low, 8)
+            return self.ref.at[turn(self.place, 4 - k), pl.ds(at_row, count)]
+
+        def quarter(self, k, q):
+            return self.rows(k, q * self.piece, self.piece, c)
+
+        def half(self, k, p, which):
+            return self.rows(k, p * 2 * self.piece, 2 * self.piece, which)
 
         def start(self):
-            for k, p in ((1, 0), (3, 1), (1, 1), (3, 0)):
-                start(self.part(0, p, c), self.part(0, p, c), self.first[k, p], self.peers[k])
+            for k, q in self.handed:
+                start(self.quarter(0, q), self.quarter(0, q), self.first[k, q], self.peers[k])
+            for k, p in ((1, 1), (3, 0)):
+                start(self.half(0, p, c), self.half(0, p, c), self.first[k, "rest"], self.peers[k])
 
         def inside(self, k, p):
-            start(self.part(k, p, c), self.part(k, p, c), self.second[k, p], sibling)
+            start(self.half(k, p, c), self.half(k, p, c), self.second[k, p], sibling)
 
         def relay(self):
-            for k, p in ((1, 0), (3, 1)):
-                arrived(self.part(k, p, c), self.first[k, p])
-                start(self.part(k, p, c), self.part(k, p, c), self.first[2, p], self.peers[k])
-            for k, p in ((1, 0), (3, 1)):
+            for k, q in self.handed:
+                arrived(self.quarter(k, q), self.first[k, q])
+                start(self.quarter(k, q), self.quarter(k, q), self.far[k, q], self.peers[k])
+            self.inside(1, 0)
+            self.inside(3, 1)
+
+        def forward(self):
+            for k, p in ((1, 1), (3, 0)):
+                arrived(self.half(k, p, c), self.first[k, "rest"])
                 self.inside(k, p)
-
-        def forward(self):
-            for k, p in ((1, 1), (3, 0), (2, 0), (2, 1)):
-                arrived(self.part(k, p, c), self.first[k, p])
-                self.inside(k, p)
+            for k, q in self.handed:
+                arrived(self.quarter(2, q), self.far[k, q])
+            start(self.rows(2, 0, HALF, c), self.rows(2, 0, HALF, c), self.second[2, None], sibling)
 
         def finish(self):
             for k, p in self.second:
-                arrived(self.part(k, p, 1 - c), self.second[k, p])
+                part = self.rows(2, 0, HALF, 1 - c) if p is None else self.half(k, p, 1 - c)
+                arrived(part, self.second[k, p])
 
     class Share:
         def __init__(self, ref, place, peers):
@@ -264,7 +278,7 @@
     own0[...] = dot(pack(-upper[1], sketch[1]), inv_diag[1])
     y1s[...] = compose(y0s[...], own0[...])
     fc[c] = y1s[...]
-    pl.semaphore_wait(barrier, 1 + 3 + 15)
+    pl.semaphore_wait(barrier, 1 + 3 + 3 + 15)
     sem_f, sem_g, sem_h = slot(), slot(), slot()
     swap(fc, sem_f)
     for i in (4, 5):
@@ -432,16 +446,17 @@
     gram = jnp.concatenate([gram[0 : K // 2], gram[K // 2 : K]], axis=1)
     gown[0] = gram[0 : K // 4]
     gown[1] = gram[K // 4 : K // 2]
-    sem_gin, sem_gtot = slot(), slot()
-    start(gown.at[1 - c], gin, sem_gin, sibling)
-    arrived(gin, sem_gin)
-    gx[x] = gown[c] + gin[...]
-    share_gx = Share(gx, x, xs)
-    share_gx.start()
+    mates = {(k, f): slot() for k in (1, 3, 2, 0) for f in (1, 0) if (k, f) != (0, 0)}
+    here = x * 2 + c
+    for (k, f), i in mates.items():
+        other = c if f == 0 else 1 - c
+        start(gown.at[other], gx.at[here], i, at(z, y, turn(x, k), other))
+    gx[here] = gown[c]
     drain(9)
-    share_gx.finish()
+    for (k, f), i in mates.items():
+        arrived(gx.at[turn(x, 4 - k) * 2 + (c if f == 0 else 1 - c)], i)
     own = z * 4 + y
-    gyz[own] = (gx[0] + gx[1]) + (gx[2] + gx[3])
+    gyz[own] = ((gx[0] + gx[1]) + (gx[2] + gx[3])) + ((gx[4] + gx[5]) + (gx[6] + gx[7]))
     sems = {step: slot() for step in across}
     for step, other in across.items():
         start(gyz.at[own], gyz.at[own], sems[step], other)
@@ -452,6 +467,7 @@
     while len(terms) > 1:
         terms = [terms[i] + terms[i + 1] for i in range(0, len(terms), 2)]
     gtot[c] = terms[0]
+    sem_gtot = slot()
     swap(gtot, sem_gtot)
     drain(15)
     arrived(gtot.at[1 - c], sem_gtot)
@@ -478,12 +494,12 @@
         buf(4, *affine), buf(4, W, W), buf(4, *affine), buf(4, W, W), buf(3, W, W), buf(*affine),
         buf(*affine), buf(*part), buf(W, W), buf(*part), buf(2, *part), buf(4, W, W), buf(2, *part),
         buf(4, *part), buf(4, *part), buf(4, *part), buf(2, *part), buf(2, *part),
-        buf(2, *quarter), buf(*quarter), buf(4, *quarter), buf(16, *quarter), buf(2, *quarter),
+        buf(2, *quarter), buf(8, *quarter), buf(16, *quarter), buf(2, *quarter),
         pltpu.SemaphoreType.DMA((SEMS,)), pltpu.SemaphoreType.DMA((SEMS,)), pltpu.SemaphoreType.DMA((7,)),
     ]
     return pl.pallas_call(
         kernel,
-        out_shape=(jax.ShapeDtypeStruct((2, K, W), F32), jax.ShapeDtypeStruct((K, K), F32)),
+        out_shape=(pltpu.VMEM((2, K, W), F32), pltpu.VMEM((K, K), F32)),
         in_specs=[pl.BlockSpec(memory_space=pl.ANY)] * 4,
         out_specs=(vmem, vmem),
         scratch_shapes=scratch,

time: 72.9 us -> 70 us (0.960)
  Pallas kernels: 69.9 us -> 68 us
  local copies, waits for them, and re-layouts: 2.19 us -> 1.27 us
    pallas_call x1, Pallas kernels: 69.9 us -> 68 us  [on_device(): pl.pallas_call(kernel, out_shape=(pltpu.VMEM((2, K, W), F32), pltpu.VMEM(...]
    unnamed x4 -> x2, local copies, waits for them, and re-layouts: 2.19 us -> 1.27 us
where the time goes in v5:
time: 70 us; the launch traced here: 69.9 us
  Pallas kernels  68 us (97%)
  local copies, waits for them, and re-layouts  1.27 us (2%)
    pallas_call x1, Pallas kernels, on_device(): pl.pallas_call(kernel, out_shape=(pltpu.VMEM((2, K, W), F32), pltpu.VMEM(...  68 us

profile of v5, /device:TPU:1, one launch (start us, length us, event | category | flops | bytes accessed | tf_op | source)
XLA Modules:
  0.0 69.9 jit_solution(10864120406822597173)
XLA Ops:
  0.6 68.0 %sweeps.1 = (f32[2,64,256]{2,1,0:T(8,128)S(1)}, f32[64,64]{1,0:T(8,128)S(1)}) custom-call(f32[2,64,256]{2,1,0:T(8,128)} %sketch_in.1, f32[2,256,256]{2,1,0:T(8,128)} %inv_diag_in.1, f32[2,256,256]{2,1,0:T(8,128)} %upper_in.1, f32[2,256,256]{2,1,0:T(8,128)} %lower_in.1), custom_call_target="tpu_custom_call" | custom-call | tf_op jit(solution)/shard_map/sweeps/pallas_call | solution.py:500
  68.6 0.7 copy.8
  69.3 0.6 copy.9

commit v6 on v5

--- a/solution.py
+++ b/solution.py
@@ -129,12 +129,13 @@
 
     sibling = at(z, y, x, 1 - c)
     xs = [at(z, y, turn(x, k), c) for k in range(4)]
-    across = {(k, n): at(turn(z, k), turn(y, n), x, c) for k in (0, 1, 3, 2) for n in (0, 1, 3, 2) if (k, n) != (0, 0)}
+    steps = sorted(((k, n) for k in range(4) for n in range(4)), key=lambda s: -sum(min(v, 4 - v) for v in s))
+    across = {(k, n): at(turn(z, k), turn(y, n), x, c) for k, n in steps if (k, n) != (0, 0)}
     ys = [None, *(across[0, n] for n in (1, 2, 3))]
     zs = [None, *(across[k, 0] for k in (1, 2, 3))]
 
     barrier = pltpu.get_barrier_semaphore()
-    for other in (sibling, *xs[1:], *(at(z, y, turn(x, k), 1 - c) for k in (1, 2, 3)), *across.values()):
+    for other in (*zs[1:], *ys[1:], *xs[1:], sibling):
         pl.semaphore_signal(barrier, inc=1, device_id=(other,), device_id_type=MESH)
 
     sent = []
@@ -260,7 +261,7 @@
             self.sems = {k: slot() for k in (1, 3, 2)}
 
         def start(self):
-            for k in (1, 3, 2):
+            for k in (2, 1, 3):
                 start(self.ref.at[self.place], self.ref.at[self.place], self.sems[k], self.peers[k])
 
         def finish(self):
@@ -278,7 +279,7 @@
     own0[...] = dot(pack(-upper[1], sketch[1]), inv_diag[1])
     y1s[...] = compose(y0s[...], own0[...])
     fc[c] = y1s[...]
-    pl.semaphore_wait(barrier, 1 + 3 + 3 + 15)
+    pl.semaphore_wait(barrier, 1 + 3 + 3 + 3)
     sem_f, sem_g, sem_h = slot(), slot(), slot()
     swap(fc, sem_f)
     for i in (4, 5):
@@ -336,10 +337,10 @@
     xsuf_g[3] = eye
     xsuf_g[2] = xg[3]
     xsuf_g[1] = dot(xg[3], xg[2])
-    xsuf_g[0] = dot(xsuf_g[1], xg[1])
-    yg[y] = dot(xsuf_g[0], xg[0])
+    yg[y] = dot(xsuf_g[1], dot(xg[1], xg[0]))
     gather_yg = Gather(yg, HALF_M, y, ys, (1, 3, 2))
     gather_yg.start()
+    xsuf_g[0] = dot(xsuf_g[1], xg[1])
     gather_yf.forward()
     gather_yf.finish()
     q23 = compose(yf[2], yf[3])
@@ -366,8 +367,8 @@
 
     arrived(zc_in, sem_c)
     va[...] = dot(zc_in[...], mat(zf[...])) + zf[my_vec]
+    start(va, va_in.at[1], sem_v2, zs[2])
     start(va, va_in.at[0], sem_v1, zs[1])
-    start(va, va_in.at[1], sem_v2, zs[2])
     arrived(zm_in.at[my_half], sem_m)
     start(zm_in.at[my_half], zm_in.at[my_half], sem_m2, sibling)
 
@@ -392,23 +393,18 @@
     gather_yg.finish()
     ysuf_g[3] = eye
     ysuf_g[2] = yg[3]
+    ysum[1] = dot(yg[1], yg[0])
     ysuf_g[1] = dot(yg[3], yg[2])
-    ysuf_g[0] = dot(ysuf_g[1], yg[1])
-    zg[z] = dot(ysuf_g[0], yg[0])
+    zg[z] = dot(ysuf_g[1], ysum[1])
     gather_zg = Gather(zg, HALF_M, z, zs, (3, 2), ((z == 1) | (z == 2), z == 2), (z < 2, z == 0))
     gather_zg.start()
 
     ysum[0] = yg[0]
-    ysum[1] = dot(yg[1], yg[0])
     ysum[2] = dot(yg[2], ysum[1])
+    ysuf_g[0] = dot(ysuf_g[1], yg[1])
 
     dev_h[...] = dot(xsuf_h[x], dev_g[...]) + dev_h[...]
     dev_g[...] = dot(xsuf_g[x], dev_g[...])
-    arrived(entry.at[1 - c], sem_entry)
-    row = apply(jnp.concatenate([entry[0], entry[1]], axis=0), ypre[y])
-    x1 = apply(row, y1s[...]) - apply(row, dev_h[...])
-    x0 = apply(row, y0s[...]) - dot(x1, lower[1])
-
     share_er.finish()
     ep[z] = dot(jnp.concatenate([er[1], er[2], er[3]], axis=1), ysum[...].reshape(3 * W, W)) + er[0]
 
@@ -421,6 +417,10 @@
     ends[c] = ysuf_e[y]
     sem_ends = slot()
     swap(ends, sem_ends)
+    arrived(entry.at[1 - c], sem_entry)
+    row = apply(jnp.concatenate([entry[0], entry[1]], axis=0), ypre[y])
+    x1 = apply(row, y1s[...]) - apply(row, dev_h[...])
+    x0 = apply(row, y0s[...]) - dot(x1, lower[1])
     to_w1 = dot(ysuf_g[y], dev_g[...])
     to_w0 = dot(to_w1, lower[1])
     arrived(ends.at[1 - c], sem_ends)
@@ -446,7 +446,7 @@
     gram = jnp.concatenate([gram[0 : K // 2], gram[K // 2 : K]], axis=1)
     gown[0] = gram[0 : K // 4]
     gown[1] = gram[K // 4 : K // 2]
-    mates = {(k, f): slot() for k in (1, 3, 2, 0) for f in (1, 0) if (k, f) != (0, 0)}
+    mates = {(k, f): slot() for k in (2, 1, 3, 0) for f in (1, 0) if (k, f) != (0, 0)}
     here = x * 2 + c
     for (k, f), i in mates.items():
         other = c if f == 0 else 1 - c

time: 70 us -> 67.7 us (0.967)
  Pallas kernels: 68 us -> 65.7 us
    pallas_call x1, Pallas kernels: 68 us -> 65.7 us  [on_device(): pl.pallas_call(kernel, out_shape=(pltpu.VMEM((2, K, W), F32), pltpu.VMEM(...]
where the time goes in v6:
time: 67.7 us; the launch traced here: 67.6 us
  Pallas kernels  65.7 us (97%)
  local copies, waits for them, and re-layouts  1.27 us (2%)
    pallas_call x1, Pallas kernels, on_device(): pl.pallas_call(kernel, out_shape=(pltpu.VMEM((2, K, W), F32), pltpu.VMEM(...  65.7 us

profile of v6, /device:TPU:1, one launch (start us, length us, event | category | flops | bytes accessed | tf_op | source)
XLA Modules:
  0.0 67.6 jit_solution(6079016923829273383)
XLA Ops:
  0.6 65.7 %sweeps.1 = (f32[2,64,256]{2,1,0:T(8,128)S(1)}, f32[64,64]{1,0:T(8,128)S(1)}) custom-call(f32[2,64,256]{2,1,0:T(8,128)} %sketch_in.1, f32[2,256,256]{2,1,0:T(8,128)} %inv_diag_in.1, f32[2,256,256]{2,1,0:T(8,128)} %upper_in.1, f32[2,256,256]{2,1,0:T(8,128)} %lower_in.1), custom_call_target="tpu_custom_call" | custom-call | tf_op jit(solution)/shard_map/sweeps/pallas_call | solution.py:500
  66.3 0.7 copy.8
  66.9 0.6 copy.9

commit v7 on v6

--- a/solution.py
+++ b/solution.py
@@ -105,7 +105,7 @@
     sketch, inv_diag, upper, lower, own0, fc, gc, hc, y0s, y1s, dev_g, dev_h,
     xf, xg, xh, xpre, xsuf_h, xsuf_g, yf, yg, ypre, ysuf_g, ysum, row_h,
     zf, zc_in, zm_in, va, va_in, zg, entry, er, ep, ysuf_e, ends, tops, gown, gx, gyz, gtot,
-    send, recv, load,
+    send, recv, load, heard,
 ):
     me = lax.axis_index("chain")
     c = lax.rem(me, 2)
@@ -135,8 +135,15 @@
     zs = [None, *(across[k, 0] for k in (1, 2, 3))]
 
     barrier = pltpu.get_barrier_semaphore()
-    for other in (*zs[1:], *ys[1:], *xs[1:], sibling):
+    above, below = z < 3, z > 0
+
+    def greet(other):
         pl.semaphore_signal(barrier, inc=1, device_id=(other,), device_id_type=MESH)
+
+    pl.when(above)(lambda: greet(zs[1]))
+    pl.when(below)(lambda: greet(zs[3]))
+    for other in (ys[1], ys[3], xs[1], xs[3], sibling):
+        greet(other)
 
     sent = []
     used = [0]
@@ -256,17 +263,19 @@
                 arrived(part, self.second[k, p])
 
     class Share:
-        def __init__(self, ref, place, peers):
+        def __init__(self, ref, place, peers, gives=None, takes=None):
             self.ref, self.place, self.peers = ref, place, peers
+            self.gives, self.takes = gives or {}, takes or {}
             self.sems = {k: slot() for k in (1, 3, 2)}
 
         def start(self):
+            own = self.ref.at[self.place]
             for k in (2, 1, 3):
-                start(self.ref.at[self.place], self.ref.at[self.place], self.sems[k], self.peers[k])
+                start(own, own, self.sems[k], self.peers[k], self.gives.get(k))
 
         def finish(self):
             for k in (1, 3, 2):
-                arrived(self.ref.at[turn(self.place, 4 - k)], self.sems[k])
+                arrived(self.ref.at[turn(self.place, 4 - k)], self.sems[k], self.takes.get(k))
 
     def swap(ref, i):
         start(ref.at[c], ref.at[c], i, sibling)
@@ -279,7 +288,8 @@
     own0[...] = dot(pack(-upper[1], sketch[1]), inv_diag[1])
     y1s[...] = compose(y0s[...], own0[...])
     fc[c] = y1s[...]
-    pl.semaphore_wait(barrier, 1 + 3 + 3 + 3)
+    pl.semaphore_wait(barrier, 5 + jnp.where(above, 1, 0) + jnp.where(below, 1, 0))
+    pl.when(z == 2)(lambda: pl.semaphore_signal(heard, inc=1, device_id=(zs[3],), device_id_type=MESH))
     sem_f, sem_g, sem_h = slot(), slot(), slot()
     swap(fc, sem_f)
     for i in (4, 5):
@@ -349,12 +359,13 @@
     zf[my_vec] = dot(ypre[2, my_vec], mat(q23)) + xsuf_h[0, my_vec]
 
     sem_c, sem_m, sem_m2, sem_v1, sem_v2 = slot(), slot(), slot(), slot(), slot()
-    start(zf.at[my_vec], zc_in, sem_c, zs[1])
+    even, odd = lax.rem(z, 2) == 0, lax.rem(z, 2) == 1
+    start(zf.at[my_vec], zc_in, sem_c, zs[1], even)
     my_m = pl.ds(pl.multiple_of(c * HALF, 8), HALF_M)
     other_m = pl.ds(pl.multiple_of((1 - c) * HALF, 8), HALF_M)
     my_half, other_half = rows_of(c, HALF_M), rows_of(1 - c, HALF_M)
     zf[my_m] = dot(ypre[2, my_m], mat(q23))
-    start(zf.at[my_m], zm_in.at[my_half], sem_m, zs[1])
+    start(zf.at[my_m], zm_in.at[my_half], sem_m, zs[1], z == 2)
     ypre[2, others] = compose_half(yf[0, others], yf.at[1], 1 - c)
     zf[other_m] = dot(ypre[2, other_m], mat(q23))
     gather_xh.forward()
@@ -365,21 +376,27 @@
     xsuf_h[2] = compose(xpre[3], xh[3])
     xsuf_h[1] = dot(xsuf_h[2], xg[2]) + compose(xpre[2], xh[2])
 
-    arrived(zc_in, sem_c)
-    va[...] = dot(zc_in[...], mat(zf[...])) + zf[my_vec]
-    start(va, va_in.at[1], sem_v2, zs[2])
-    start(va, va_in.at[0], sem_v1, zs[1])
-    arrived(zm_in.at[my_half], sem_m)
-    start(zm_in.at[my_half], zm_in.at[my_half], sem_m2, sibling)
+    arrived(zc_in, sem_c, z == 1)
+
+    @pl.when(z == 1)
+    def _():
+        pl.semaphore_wait(heard, 1)
+        va[...] = dot(zc_in[...], mat(zf[...])) + zf[my_vec]
+
+    start(va, va_in.at[1], sem_v2, zs[2], z == 1)
+    start(va, va_in.at[0], sem_v1, zs[1], z == 1)
+    arrived(zm_in.at[my_half], sem_m, z == 3)
+    start(zm_in.at[my_half], zm_in.at[my_half], sem_m2, sibling, z == 3)
 
     ypre[3] = compose(ypre[2], yf[2])
     xsuf_h[0] = dot(xsuf_h[1], xg[1]) + compose(xf[0], xh[1])
     row_h[...] = compose(ypre[y], dot(xsuf_h[0], xg[0]) + xh[0])
     drain(24)
 
-    arrived(zm_in.at[other_half], sem_m2)
-    arrived(va_in.at[0], sem_v1)
-    arrived(va_in.at[1], sem_v2)
+    arrived(zc_in, sem_c, z == 3)
+    arrived(zm_in.at[other_half], sem_m2, z == 3)
+    arrived(va_in.at[0], sem_v1, z == 2)
+    arrived(va_in.at[1], sem_v2, z == 3)
     last = dot(va_in[1], zm_in[...]) + zc_in[...]
     start_row = jnp.where(z == 0, 0.0, jnp.where(z == 1, zc_in[...], jnp.where(z == 2, va_in[0], last)))
 
@@ -408,7 +425,7 @@
     share_er.finish()
     ep[z] = dot(jnp.concatenate([er[1], er[2], er[3]], axis=1), ysum[...].reshape(3 * W, W)) + er[0]
 
-    share_ep = Share(ep, z, zs)
+    share_ep = Share(ep, z, zs, {1: z == 3, 2: z >= 2, 3: z >= 1}, {1: z == 0, 2: z <= 1, 3: z <= 2})
     share_ep.start()
     ysuf_e[3] = jnp.zeros((HALF_C, W), F32)
     ysuf_e[2] = er[3]
@@ -496,6 +513,7 @@
         buf(4, *part), buf(4, *part), buf(4, *part), buf(2, *part), buf(2, *part),
         buf(2, *quarter), buf(8, *quarter), buf(16, *quarter), buf(2, *quarter),
         pltpu.SemaphoreType.DMA((SEMS,)), pltpu.SemaphoreType.DMA((SEMS,)), pltpu.SemaphoreType.DMA((7,)),
+        pltpu.SemaphoreType.REGULAR,
     ]
     return pl.pallas_call(
         kernel,

time: 67.7 us -> 65.4 us (0.966)
  Pallas kernels: 65.7 us -> 63.3 us
    pallas_call x1, Pallas kernels: 65.7 us -> 63.3 us  [on_device(): pl.pallas_call(kernel, out_shape=(pltpu.VMEM((2, K, W), F32), pltpu.VMEM(...]
where the time goes in v7:
time: 65.4 us; the launch traced here: 65.3 us
  Pallas kernels  63.3 us (97%)
  local copies, waits for them, and re-layouts  1.27 us (2%)
    pallas_call x1, Pallas kernels, on_device(): pl.pallas_call(kernel, out_shape=(pltpu.VMEM((2, K, W), F32), pltpu.VMEM(...  63.3 us

profile of v7, /device:TPU:1, one launch (start us, length us, event | category | flops | bytes accessed | tf_op | source)
XLA Modules:
  0.0 65.3 jit_solution(678426407775315397)
XLA Ops:
  0.6 63.3 %sweeps.1 = (f32[2,64,256]{2,1,0:T(8,128)S(1)}, f32[64,64]{1,0:T(8,128)S(1)}) custom-call(f32[2,64,256]{2,1,0:T(8,128)} %sketch_in.1, f32[2,256,256]{2,1,0:T(8,128)} %inv_diag_in.1, f32[2,256,256]{2,1,0:T(8,128)} %upper_in.1, f32[2,256,256]{2,1,0:T(8,128)} %lower_in.1), custom_call_target="tpu_custom_call" | custom-call | tf_op jit(solution)/shard_map/sweeps/pallas_call | solution.py:518
  64.0 0.7 %copy.8 = f32[2,64,256]{2,1,0:T(8,128)} copy(f32[2,64,256]{2,1,0:T(8,128)S(1)} %get-tuple-element.2) | data formatting | bytes 262144
  64.6 0.6 copy.9

commit v8 on v7

--- a/solution.py
+++ b/solution.py
@@ -221,7 +221,7 @@
             self.ref, self.place, self.peers = ref, place, peers
             self.first = {key: slot() for key in (*self.handed, (1, "rest"), (3, "rest"))}
             self.far = {key: slot() for key in self.handed}
-            self.second = {key: slot() for key in ((1, 0), (3, 1), (1, 1), (3, 0), (2, None))}
+            self.second = {key: slot() for key in ((1, 0), (3, 1), (1, 1), (3, 0), (2, 0), (2, 1))}
 
         def rows(self, k, low, count, which):
             at_row = pl.multiple_of(which * HALF + low, 8)
@@ -253,14 +253,14 @@
             for k, p in ((1, 1), (3, 0)):
                 arrived(self.half(k, p, c), self.first[k, "rest"])
                 self.inside(k, p)
-            for k, q in self.handed:
-                arrived(self.quarter(2, q), self.far[k, q])
-            start(self.rows(2, 0, HALF, c), self.rows(2, 0, HALF, c), self.second[2, None], sibling)
+            for k, p in ((1, 0), (3, 1)):
+                for q in (2 * p, 2 * p + 1):
+                    arrived(self.quarter(2, q), self.far[k, q])
+                self.inside(2, p)
 
         def finish(self):
             for k, p in self.second:
-                part = self.rows(2, 0, HALF, 1 - c) if p is None else self.half(k, p, 1 - c)
-                arrived(part, self.second[k, p])
+                arrived(self.half(k, p, 1 - c), self.second[k, p])
 
     class Share:
         def __init__(self, ref, place, peers, gives=None, takes=None):
@@ -313,6 +313,8 @@
     arrived(hc.at[1 - c], sem_h)
     late = compose(fc[0], hc[1])
     xh[x] = dot(late, gc[0]) + hc[0]
+    gather_xh = Gather(xh, HALF, x, xs, (1, 3, 2))
+    gather_xh.start()
     second = c == 1
     eye = identity(W, W)
     dev_g[...] = jnp.where(second, eye, gc[1])
@@ -329,8 +331,6 @@
 
     gather_yf = Relay(yf, y, ys)
     gather_yf.start()
-    gather_xh = Gather(xh, HALF, x, xs, (1, 3, 2))
-    gather_xh.start()
     xpre[2, others] = compose_half(xf[0, others], xf.at[1], 1 - c)
     yf[y, others] = compose_half(xpre[2, others], xsuf_h.at[0], 1 - c)
     xpre[0] = pack(eye, jnp.zeros((K, W), F32))
@@ -393,6 +393,7 @@
     row_h[...] = compose(ypre[y], dot(xsuf_h[0], xg[0]) + xh[0])
     drain(24)
 
+    gather_yg.forward()
     arrived(zc_in, sem_c, z == 3)
     arrived(zm_in.at[other_half], sem_m2, z == 3)
     arrived(va_in.at[0], sem_v1, z == 2)
@@ -406,7 +407,6 @@
     entry[c] = start_row
     sem_entry = slot()
     swap(entry, sem_entry)
-    gather_yg.forward()
     gather_yg.finish()
     ysuf_g[3] = eye
     ysuf_g[2] = yg[3]

time: 65.4 us -> 65.2 us (level)
  no operation moved by 1% of the time
where the time goes in v8:
time: 65.2 us; the launch traced here: 65 us
  Pallas kernels  63.1 us (97%)
  local copies, waits for them, and re-layouts  1.27 us (2%)
    pallas_call x1, Pallas kernels, on_device(): pl.pallas_call(kernel, out_shape=(pltpu.VMEM((2, K, W), F32), pltpu.VMEM(...  63.1 us

profile of v8, /device:TPU:1, one launch (start us, length us, event | category | flops | bytes accessed | tf_op | source)
XLA Modules:
  0.0 65.0 jit_solution(3620326653131237033)
XLA Ops:
  0.6 63.1 %sweeps.1 = (f32[2,64,256]{2,1,0:T(8,128)S(1)}, f32[64,64]{1,0:T(8,128)S(1)}) custom-call(f32[2,64,256]{2,1,0:T(8,128)} %sketch_in.1, f32[2,256,256]{2,1,0:T(8,128)} %inv_diag_in.1, f32[2,256,256]{2,1,0:T(8,128)} %upper_in.1, f32[2,256,256]{2,1,0:T(8,128)} %lower_in.1), custom_call_target="tpu_custom_call" | custom-call | tf_op jit(solution)/shard_map/sweeps/pallas_call | solution.py:518
  63.8 0.7 %copy.8 = f32[2,64,256]{2,1,0:T(8,128)} copy(f32[2,64,256]{2,1,0:T(8,128)S(1)} %get-tuple-element.2) | data formatting | bytes 262144
  64.4 0.6 copy.9

commit v9 on v8

--- a/solution.py
+++ b/solution.py
@@ -103,7 +103,7 @@
 def kernel(
     sketch_in, inv_diag_in, upper_in, lower_in, basis, r_factor,
     sketch, inv_diag, upper, lower, own0, fc, gc, hc, y0s, y1s, dev_g, dev_h,
-    xf, xg, xh, xpre, xsuf_h, xsuf_g, yf, yg, ypre, ysuf_g, ysum, row_h,
+    xf, xg, xh, xpre, xsuf_h, xsuf_g, yf, yg, ypre, ysuf_g, ysum, row_h, pairs_x, pairs_y,
     zf, zc_in, zm_in, va, va_in, zg, entry, er, ep, ysuf_e, ends, tops, gown, gx, gyz, gtot,
     send, recv, load, heard,
 ):
@@ -258,9 +258,16 @@
                     arrived(self.quarter(2, q), self.far[k, q])
                 self.inside(2, p)
 
-        def finish(self):
-            for k, p in self.second:
-                arrived(self.half(k, p, 1 - c), self.second[k, p])
+        def finish(self, pairs):
+            def pair(i):
+                pairs[i] = compose(self.ref[2 * i], self.ref[2 * i + 1])
+
+            own_pair = self.place // 2
+            for far in (False, True):
+                for k, p in self.second:
+                    if (k == 2) == far:
+                        arrived(self.half(k, p, 1 - c), self.second[k, p])
+                pair(1 - own_pair if far else own_pair)
 
     class Share:
         def __init__(self, ref, place, peers, gives=None, takes=None):
@@ -323,16 +330,13 @@
     y1s[...] = jnp.where(second, xf[x], y1s[...])
     drain(3)
     gather_xf.forward()
-    gather_xf.finish()
-    q23 = compose(xf[2], xf[3])
-    xsuf_h[0] = q23
-    xpre[2, mine] = compose_half(xf[0, mine], xf.at[1], c)
-    yf[y, mine] = compose_half(xpre[2, mine], xsuf_h.at[0], c)
+    gather_xf.finish(pairs_x)
+    yf[y, mine] = compose_half(pairs_x[0, mine], pairs_x.at[1], c)
 
     gather_yf = Relay(yf, y, ys)
     gather_yf.start()
-    xpre[2, others] = compose_half(xf[0, others], xf.at[1], 1 - c)
-    yf[y, others] = compose_half(xpre[2, others], xsuf_h.at[0], 1 - c)
+    xpre[2] = pairs_x[0]
+    yf[y, others] = compose_half(pairs_x[0, others], pairs_x.at[1], 1 - c)
     xpre[0] = pack(eye, jnp.zeros((K, W), F32))
     xpre[1] = xf[0]
     xpre[3] = compose(xpre[2], xf[2])
@@ -352,11 +356,9 @@
     gather_yg.start()
     xsuf_g[0] = dot(xsuf_g[1], xg[1])
     gather_yf.forward()
-    gather_yf.finish()
-    q23 = compose(yf[2], yf[3])
-    xsuf_h[0] = q23
-    ypre[2, mine] = compose_half(yf[0, mine], yf.at[1], c)
-    zf[my_vec] = dot(ypre[2, my_vec], mat(q23)) + xsuf_h[0, my_vec]
+    gather_yf.finish(pairs_y)
+    ypre[2] = pairs_y[0]
+    zf[my_vec] = dot(pairs_y[0, my_vec], mat(pairs_y[1])) + pairs_y[1, my_vec]
 
     sem_c, sem_m, sem_m2, sem_v1, sem_v2 = slot(), slot(), slot(), slot(), slot()
     even, odd = lax.rem(z, 2) == 0, lax.rem(z, 2) == 1
@@ -364,10 +366,9 @@
     my_m = pl.ds(pl.multiple_of(c * HALF, 8), HALF_M)
     other_m = pl.ds(pl.multiple_of((1 - c) * HALF, 8), HALF_M)
     my_half, other_half = rows_of(c, HALF_M), rows_of(1 - c, HALF_M)
-    zf[my_m] = dot(ypre[2, my_m], mat(q23))
+    zf[my_m] = dot(pairs_y[0, my_m], mat(pairs_y[1]))
     start(zf.at[my_m], zm_in.at[my_half], sem_m, zs[1], z == 2)
-    ypre[2, others] = compose_half(yf[0, others], yf.at[1], 1 - c)
-    zf[other_m] = dot(ypre[2, other_m], mat(q23))
+    zf[other_m] = dot(pairs_y[0, other_m], mat(pairs_y[1]))
     gather_xh.forward()
     ypre[0] = pack(eye, jnp.zeros((K, W), F32))
     ypre[1] = yf[0]
@@ -508,7 +509,7 @@
         buf(2, K, W), buf(2, W, W), buf(2, W, W), buf(2, W, W), buf(*affine), buf(2, *affine), buf(2, W, W), buf(2, *affine),
         buf(*affine), buf(*affine), buf(W, W), buf(*affine),
         buf(4, *affine), buf(4, W, W), buf(4, *affine), buf(4, *affine), buf(4, *affine), buf(4, W, W),
-        buf(4, *affine), buf(4, W, W), buf(4, *affine), buf(4, W, W), buf(3, W, W), buf(*affine),
+        buf(4, *affine), buf(4, W, W), buf(4, *affine), buf(4, W, W), buf(3, W, W), buf(*affine), buf(2, *affine), buf(2, *affine),
         buf(*affine), buf(*part), buf(W, W), buf(*part), buf(2, *part), buf(4, W, W), buf(2, *part),
         buf(4, *part), buf(4, *part), buf(4, *part), buf(2, *part), buf(2, *part),
         buf(2, *quarter), buf(8, *quarter), buf(16, *quarter), buf(2, *quarter),

time: 65.2 us -> 65.8 us (level)
  no operation moved by 1% of the time
where the time goes in v9:
time: 65.8 us; the launch traced here: 65.6 us
  Pallas kernels  63.7 us (97%)
  local copies, waits for them, and re-layouts  1.27 us (2%)
    pallas_call x1, Pallas kernels, on_device(): pl.pallas_call(kernel, out_shape=(pltpu.VMEM((2, K, W), F32), pltpu.VMEM(...  63.7 us

profile of v9, /device:TPU:1, one launch (start us, length us, event | category | flops | bytes accessed | tf_op | source)
XLA Modules:
  0.0 65.6 jit_solution(6189060426067577140)
XLA Ops:
  0.6 63.7 %sweeps.1 = (f32[2,64,256]{2,1,0:T(8,128)S(1)}, f32[64,64]{1,0:T(8,128)S(1)}) custom-call(f32[2,64,256]{2,1,0:T(8,128)} %sketch_in.1, f32[2,256,256]{2,1,0:T(8,128)} %inv_diag_in.1, f32[2,256,256]{2,1,0:T(8,128)} %upper_in.1, f32[2,256,256]{2,1,0:T(8,128)} %lower_in.1), custom_call_target="tpu_custom_call" | custom-call | tf_op jit(solution)/shard_map/sweeps/pallas_call | solution.py:519
  64.4 0.7 %copy.8 = f32[2,64,256]{2,1,0:T(8,128)} copy(f32[2,64,256]{2,1,0:T(8,128)S(1)} %get-tuple-element.2) | data formatting | bytes 262144
  65.0 0.6 copy.9
